TPU v7x, 32 devices: a whole 2x2x4 slice. The times are simulated.
32 devices in a mesh: dp: 8 (over y, x, core), tensor: 4 (over z).
Axes of the slice: x: 2, y: 2, z: 4, core: 2. Of those that a mesh axis runs over, the one named last changes fastest.
Arguments:
- inputs: bfloat16 [2, 16384, 768], P(None, 'dp'), may hold values from -6 to 6
- cotangent: bfloat16 [2, 16384, 768], P(None, 'dp'), may hold values from -6 to 6
- bucket: int32 [2, 32], P(None, 'dp'), may hold values from 0 to 1, as said below
- lengths: int32 [2, 32, 4], P(None, 'dp'), may hold values from 64 to 512, as said below
- counts: int32 [2, 32], P(None, 'dp'), may hold values from 1 to 4, as said below
- w_qkv: bfloat16 [3, 768, 768], P(None, 'dp', 'tensor'), may hold values from -0.21875 to 0.21875
- w_out: bfloat16 [768, 768], P('tensor', 'dp'), may hold values from -2.5 to 2.5
- w_in: bfloat16 [768, 3072], P('dp', 'tensor'), may hold values from -0.21875 to 0.21875
- w_down: bfloat16 [3072, 768], P('tensor', 'dp'), may hold values from -0.109375 to 0.109375
- head_bias: bfloat16 [2, 768], P(None, 'tensor'), may hold values from -2 to 2
- ffn_bias: bfloat16 [3072], P('tensor'), may hold values from -2 to 2
- norm_gains: bfloat16 [2, 768], P(None, 'dp'), may hold values from 0.25 to 1.75
- row_biases: bfloat16 [4, 768], P(None, 'dp'), may hold values from -2 to 2
Outputs:
- layer_output: bfloat16 [2, 16384, 768], P(None, 'dp')
- input_grad: bfloat16 [2, 16384, 768], P(None, 'dp')
- grad_w_qkv: float32 [3, 768, 768], P(None, 'dp', 'tensor')
- grad_w_out: float32 [768, 768], P('tensor', 'dp')
- grad_w_in: float32 [768, 3072], P('dp', 'tensor')
- grad_w_down: float32 [3072, 768], P('tensor', 'dp')
- grad_head_bias: float32 [2, 768], P(None, 'tensor')
- grad_ffn_bias: float32 [3072], P('tensor')
- grad_norm_gains: float32 [2, 768], P(None, 'dp')
- grad_row_biases: float32 [4, 768], P(None, 'dp')
Inputs may be any that keep to these rules, and one draw needn't show every extreme that they name: `bucket`: 1 marks a block of one item of 512 slots, 0 a block of four items of 128 slots; every micro-batch has blocks of both kinds. `lengths`: entry i is the length of item i of the block; a one-item block uses entry 0 only, within 128 to 512; a four-item block's entries lie within 64 to 128. `counts`: 1 in a one-item block, 2 to 4 in a four-item block.
All inputs are finite; a program needn't handle non-finite values.
Results may differ from a plain program's by a relative error of at most 0.018.
Values may be sent and summed in bfloat16 or wider, within the bound.
A program may use at most 256 MiB of HBM per device.

v0:
```python
import jax
import jax.numpy as jnp
from jax import lax
from jax.sharding import PartitionSpec as P

HEAD_DIM = 64


EPSILON = 1e-12


def token_masks(bucket_id, item_lengths, item_count, slot_count):
    position = jnp.arange(slot_count, dtype=jnp.int32)
    item_size = jnp.where(bucket_id == 1, slot_count, slot_count // 4).astype(jnp.int32)
    item_index = position // item_size
    within = position % item_size
    picked = item_index[:, None] == jnp.arange(4, dtype=jnp.int32)[None, :]
    length_of = jnp.sum(jnp.where(picked, item_lengths[None, :], 0), axis=1)
    is_live = (item_index < item_count) & (within < length_of)
    keymask = (item_index[:, None] == item_index[None, :]) & is_live[None, :]
    return (is_live, keymask)


def gelu_exact(argument):
    return jax.nn.gelu(argument, approximate=False)


def norm_forward(hidden, gain_row, shift_row):
    center = hidden - jnp.mean(hidden, axis=-1, keepdims=True)
    inverse = lax.rsqrt(jnp.mean(center * center, axis=-1, keepdims=True) + EPSILON)
    normed = center * inverse
    return (normed * gain_row + shift_row, normed, inverse)


def norm_backward(grad_rows, normed, inverse, gain_row):
    grad_normed = grad_rows * gain_row
    grad_input = inverse * (
        grad_normed
        - jnp.mean(grad_normed, axis=-1, keepdims=True)
        - normed * jnp.mean(grad_normed * normed, axis=-1, keepdims=True)
    )
    return (grad_input, jnp.sum(grad_rows * normed, axis=0), jnp.sum(grad_rows, axis=0))


def block_scores(query_rows, key_rows, keymask):
    slot_count = query_rows.shape[0]
    query_heads = query_rows.reshape(slot_count, -1, HEAD_DIM)
    key_heads = key_rows.reshape(slot_count, -1, HEAD_DIM)
    scores = jnp.einsum(
        "qhd,khd->hqk", query_heads, key_heads, preferred_element_type=jnp.float32
    ) * HEAD_DIM ** (-0.5)
    return jnp.where(keymask[None], scores, -10000.0)


def add_tuples(earlier, latest):
    return tuple((first_term + second_term for first_term, second_term in zip(earlier, latest)))


def body(
    inputs,
    cotangent,
    bucket,
    lengths,
    counts,
    w_qkv,
    w_out,
    w_in,
    w_down,
    head_bias,
    ffn_bias,
    norm_gains,
    row_biases,
):
    micro_count = inputs.shape[0]
    blocks_all = bucket.shape[1]
    slot_count = inputs.shape[1] // blocks_all
    score_scale = HEAD_DIM ** (-0.5)
    fetched = (
        lax.all_gather(w_qkv, "dp", axis=1, tiled=True),
        lax.all_gather(w_out, "dp", axis=1, tiled=True),
        lax.all_gather(w_in, "dp", axis=0, tiled=True),
        lax.all_gather(w_down, "dp", axis=1, tiled=True),
        lax.all_gather(norm_gains, "dp", axis=1, tiled=True),
        lax.all_gather(row_biases, "dp", axis=1, tiled=True),
    )
    gain_rows = fetched[4].astype(jnp.float32)
    shifts = fetched[5].astype(jnp.float32)
    mat_qkv, mat_out, mat_in, mat_down = (fetched[0], fetched[1], fetched[2], fetched[3])
    column_bias = head_bias.astype(jnp.float32)
    hidden_bias = ffn_bias.astype(jnp.float32)
    row_count = blocks_all * slot_count
    share_count = row_count // lax.axis_size("tensor")
    share_start = lax.axis_index("tensor") * share_count
    results = []
    input_grads = []
    for micro_index in range(micro_count):
        tokens = inputs[micro_index]
        cot_rows = cotangent[micro_index]
        bucket_rows = bucket[micro_index]
        length_rows = lengths[micro_index]
        count_rows = counts[micro_index]
        projected = jnp.einsum("rd,tdc->trc", tokens, mat_qkv, preferred_element_type=jnp.float32)
        query_rows = (projected[0] + column_bias[0]).astype(jnp.bfloat16)
        key_rows = projected[1].astype(jnp.bfloat16)
        values = (projected[2] + column_bias[1]).astype(jnp.bfloat16)
        live_parts, mask_parts, lse_parts, context_parts = ([], [], [], [])
        for block_index in range(blocks_all):
            row_start = block_index * slot_count
            row_stop = row_start + slot_count
            is_live, keymask = token_masks(
                bucket_rows[block_index],
                length_rows[block_index],
                count_rows[block_index],
                slot_count,
            )
            scores = block_scores(
                query_rows[row_start:row_stop], key_rows[row_start:row_stop], keymask
            )
            row_peak = jnp.max(scores, axis=-1, keepdims=True)
            exp_scores = jnp.exp(scores - row_peak)
            totals = jnp.sum(exp_scores, axis=-1, keepdims=True)
            attn_probs = (exp_scores / totals).astype(jnp.bfloat16)
            value_heads = values[row_start:row_stop].reshape(slot_count, -1, HEAD_DIM)
            context = jnp.einsum(
                "hqk,khd->qhd", attn_probs, value_heads, preferred_element_type=jnp.float32
            )
            context_parts.append(context.reshape(slot_count, -1).astype(jnp.bfloat16))
            live_parts.append(is_live)
            mask_parts.append(keymask)
            lse_parts.append(row_peak + jnp.log(totals))
        context_all = jnp.concatenate(context_parts, axis=0)
        live_rows = jnp.concatenate(live_parts, axis=0).astype(jnp.float32)
        tok_share = lax.dynamic_slice_in_dim(tokens, share_start, share_count, 0).astype(
            jnp.float32
        )
        cot_share = lax.dynamic_slice_in_dim(cot_rows, share_start, share_count, 0).astype(
            jnp.float32
        )
        live_share = lax.dynamic_slice_in_dim(live_rows, share_start, share_count, 0)
        attn_partial = jnp.dot(context_all, mat_out, preferred_element_type=jnp.float32)
        attention = lax.psum_scatter(attn_partial, "tensor", scatter_dimension=0, tiled=True)
        first_norm, normed_one, inverse_one = norm_forward(
            tok_share + attention + shifts[0], gain_rows[0], shifts[1]
        )
        first_share = first_norm.astype(jnp.bfloat16)
        first_low = lax.all_gather(first_share, "tensor", axis=0, tiled=True)
        upward = jnp.dot(first_low, mat_in, preferred_element_type=jnp.float32) + hidden_bias
        activated = gelu_exact(upward).astype(jnp.bfloat16)
        down_partial = jnp.dot(activated, mat_down, preferred_element_type=jnp.float32)
        down_sum = lax.psum_scatter(down_partial, "tensor", scatter_dimension=0, tiled=True)
        result, normed_two, inverse_two = norm_forward(
            first_norm + down_sum + shifts[2], gain_rows[1], shifts[3]
        )
        grad_out = cot_share * live_share[:, None]
        grad_second, gain_two, shift_two = norm_backward(
            grad_out, normed_two, inverse_two, gain_rows[1]
        )
        second_share = grad_second.astype(jnp.bfloat16)
        second_low = lax.all_gather(second_share, "tensor", axis=0, tiled=True)
        grad_down_w = jnp.einsum(
            "rf,rd->fd", activated, second_low, preferred_element_type=jnp.float32
        )
        grad_act = jnp.einsum("rd,fd->rf", second_low, mat_down, preferred_element_type=jnp.float32)
        pullback = jax.vjp(gelu_exact, upward)[1]
        grad_up = pullback(grad_act)[0].astype(jnp.bfloat16)
        grad_in_w = jnp.einsum("rd,rf->df", first_low, grad_up, preferred_element_type=jnp.float32)
        back_partial = jnp.einsum("rf,df->rd", grad_up, mat_in, preferred_element_type=jnp.float32)
        back_total = lax.psum_scatter(back_partial, "tensor", scatter_dimension=0, tiled=True)
        grad_first = grad_second + back_total
        grad_hidden, gain_one, shift_one = norm_backward(
            grad_first, normed_one, inverse_one, gain_rows[0]
        )
        hidden_share = grad_hidden.astype(jnp.bfloat16)
        hidden_low = lax.all_gather(hidden_share, "tensor", axis=0, tiled=True)
        grad_out_w = jnp.einsum(
            "rc,rd->cd", context_all, hidden_low, preferred_element_type=jnp.float32
        )
        grad_context = jnp.einsum(
            "rd,cd->rc", hidden_low, mat_out, preferred_element_type=jnp.float32
        ).astype(jnp.bfloat16)
        query_parts, key_parts, value_parts = ([], [], [])
        for block_index in range(blocks_all):
            row_start = block_index * slot_count
            row_stop = row_start + slot_count
            keymask = mask_parts[block_index]
            scores = block_scores(
                query_rows[row_start:row_stop], key_rows[row_start:row_stop], keymask
            )
            attn_probs = jnp.exp(scores - lse_parts[block_index])
            context_heads = grad_context[row_start:row_stop].reshape(slot_count, -1, HEAD_DIM)
            value_heads = values[row_start:row_stop].reshape(slot_count, -1, HEAD_DIM)
            query_heads = query_rows[row_start:row_stop].reshape(slot_count, -1, HEAD_DIM)
            key_heads = key_rows[row_start:row_stop].reshape(slot_count, -1, HEAD_DIM)
            grad_values = jnp.einsum(
                "hqk,qhd->khd",
                attn_probs.astype(jnp.bfloat16),
                context_heads,
                preferred_element_type=jnp.float32,
            )
            grad_probs = jnp.einsum(
                "qhd,khd->hqk", context_heads, value_heads, preferred_element_type=jnp.float32
            )
            row_inner = jnp.sum(attn_probs * grad_probs, axis=-1, keepdims=True)
            grad_scores = jnp.where(
                keymask[None], attn_probs * (grad_probs - row_inner), 0.0
            ).astype(jnp.bfloat16)
            grad_query = (
                jnp.einsum(
                    "hqk,khd->qhd", grad_scores, key_heads, preferred_element_type=jnp.float32
                )
                * score_scale
            )
            grad_keys = (
                jnp.einsum(
                    "hqk,qhd->khd", grad_scores, query_heads, preferred_element_type=jnp.float32
                )
                * score_scale
            )
            query_parts.append(grad_query.reshape(slot_count, -1))
            key_parts.append(grad_keys.reshape(slot_count, -1))
            value_parts.append(grad_values.reshape(slot_count, -1))
        grad_qkv = jnp.stack(
            [
                jnp.concatenate(query_parts, axis=0),
                jnp.concatenate(key_parts, axis=0),
                jnp.concatenate(value_parts, axis=0),
            ]
        ).astype(jnp.bfloat16)
        grad_qkv_w = jnp.einsum("rd,trc->tdc", tokens, grad_qkv, preferred_element_type=jnp.float32)
        token_partial = jnp.einsum(
            "trc,tdc->rd", grad_qkv, mat_qkv, preferred_element_type=jnp.float32
        )
        token_total = lax.psum_scatter(
            token_partial.astype(jnp.bfloat16), "tensor", scatter_dimension=0, tiled=True
        ).astype(jnp.float32)
        grad_tokens = grad_hidden + token_total
        result_low = result.astype(jnp.bfloat16)
        grad_low = grad_tokens.astype(jnp.bfloat16)
        result_low, grad_low = (
            lax.all_gather(result_low, "tensor", axis=0, tiled=True),
            lax.all_gather(grad_low, "tensor", axis=0, tiled=True),
        )
        results.append(result_low)
        input_grads.append(grad_low)
        grad_qkv_wide = grad_qkv.astype(jnp.float32)
        column_grads = (
            jnp.stack([jnp.sum(grad_qkv_wide[0], axis=0), jnp.sum(grad_qkv_wide[2], axis=0)]),
            jnp.sum(grad_up.astype(jnp.float32), axis=0),
        )
        weight_grads = (
            grad_qkv_w,
            grad_out_w,
            grad_in_w,
            grad_down_w,
            jnp.stack([gain_one, gain_two]),
            jnp.stack(
                [jnp.sum(grad_hidden, axis=0), shift_one, jnp.sum(grad_second, axis=0), shift_two]
            ),
        )
        kept_weights = weight_grads if micro_index == 0 else add_tuples(kept_weights, weight_grads)
        kept_columns = column_grads if micro_index == 0 else add_tuples(kept_columns, column_grads)
    reduced = (
        lax.psum_scatter(kept_weights[0], "dp", scatter_dimension=1, tiled=True),
        lax.psum_scatter(kept_weights[1], "dp", scatter_dimension=1, tiled=True),
        lax.psum_scatter(kept_weights[2], "dp", scatter_dimension=0, tiled=True),
        lax.psum_scatter(kept_weights[3], "dp", scatter_dimension=1, tiled=True),
        lax.psum_scatter(kept_weights[4], "dp", scatter_dimension=1, tiled=True),
        lax.psum_scatter(kept_weights[5], "dp", scatter_dimension=1, tiled=True),
    )
    norm_grads = lax.psum((reduced[4], reduced[5]), "tensor")
    sent_weights = (reduced[0], reduced[1], reduced[2], reduced[3], norm_grads[0], norm_grads[1])
    sent_columns = lax.psum(kept_columns, "dp")
    return (
        jnp.stack(results),
        jnp.stack(input_grads),
        sent_weights[0],
        sent_weights[1],
        sent_weights[2],
        sent_weights[3],
        sent_columns[0],
        sent_columns[1],
        sent_weights[4],
        sent_weights[5],
    )


def solution(mesh):
    in_specs = (
        P(None, "dp", None),
        P(None, "dp", None),
        P(None, "dp"),
        P(None, "dp", None),
        P(None, "dp"),
        P(None, "dp", "tensor"),
        P("tensor", "dp"),
        P("dp", "tensor"),
        P("tensor", "dp"),
        P(None, "tensor"),
        P("tensor"),
        P(None, "dp"),
        P(None, "dp"),
    )
    out_specs = (
        P(None, "dp", None),
        P(None, "dp", None),
        P(None, "dp", "tensor"),
        P("tensor", "dp"),
        P("dp", "tensor"),
        P("tensor", "dp"),
        P(None, "tensor"),
        P("tensor"),
        P(None, "dp"),
        P(None, "dp"),
    )
    return jax.shard_map(body, mesh=mesh, in_specs=in_specs, out_specs=out_specs, check_vma=False)
```

profile of v0, /device:TPU:0, one launch (start us, length us, event | category | flops | bytes accessed | tf_op | source)
XLA Modules:
  0.0 1644.9 jit_solution(5805247536488097835)
XLA Ops:
  13.4 14.9 all_gather.48
  28.3 8.2 fusion.488
  36.6 5.0 fusion.493
  47.9 8.8 all_gather.49
  56.7 4.1 fusion.131
  97.8 6.0 fusion.476
  103.7 8.8 all-gather.1
  112.7 8.2 all-gather
  121.1 65.5 %reduce-scatter.27.cloned.1.call-done = f32[512,768]{1,0:T(8,128)} async-done(((f32[2048,768]{1,0:T(8,128)}), f32[512,768]{1,0:T(8,128)}) %reduce-scatter.27.cloned.1.call-update) | async-done | bytes 1572880 | tf_op jit(solution)/shard_map/reduce_scatter | solution.py:141
  186.6 114.2 %reduce-scatter.23.cloned.1.call-done = f32[512,768]{1,0:T(8,128)} async-done(((f32[2048,768]{1,0:T(8,128)}), f32[512,768]{1,0:T(8,128)}) %reduce-scatter.23.cloned.1.call-update) | async-done | bytes 1572880 | tf_op jit(solution)/shard_map/reduce_scatter | solution.py:141
  307.3 62.6 %all-gather.23.cloned.1.call-done = bf16[2048,768]{1,0:T(8,128)(2,1)} async-done(((bf16[512,768]{1,0:T(8,128)(2,1)}), bf16[2048,768]{1,0:T(8,128)(2,1)}) %all-gather.23.cloned.1.call-update) | async-done | bytes 3145744 | tf_op jit(solution)/shard_map/all_gather | solution.py:146
  369.9 7.5 fusion.499
  377.4 56.5 %all-gather.15.cloned.1.call-done = bf16[2048,768]{1,0:T(8,128)(2,1)} async-done(((bf16[512,768]{1,0:T(8,128)(2,1)}), bf16[2048,768]{1,0:T(8,128)(2,1)}) %all-gather.15.cloned.1.call-update) | async-done | bytes 3145744 | tf_op jit(solution)/shard_map/all_gather | solution.py:146
  433.9 33.3 %multiply_convert_fusion.1 = (bf16[2048,768]{1,0:T(8,128)(2,1)}, f32[2048,768]{1,0:T(8,128)}, bf16[2048,768]{1,0:T(8,128)(2,1)}, f32[2048,768]{1,0:T(8,128)}, f32[2048,768]{1,0:T(8,128)}) fusion(f32[768]{0:T(1024)S(1)} %convert_element_type.300, f32[2048,768]{1,0:T(8,128)} %fusion.499, bf16[2048,768]{1,0:T(8,128)(2,1)} %all-gather.15.cloned.1.call-done, ...), kind=kOutput, calls=%fused_computation.33 | convolution fusion | flops 2623537152 | bytes 35785728 | tf_op jit(solution)/shard_map/dot_general | solution.py:147
  467.2 7.5 fusion.498
  474.8 7.5 fusion.500
  483.2 5.9 fusion.475
  489.0 95.1 %reduce-scatter.25.cloned.1.call-done = f32[512,768]{1,0:T(8,128)} async-done(((f32[2048,768]{1,0:T(8,128)}), f32[512,768]{1,0:T(8,128)}) %reduce-scatter.25.cloned.1.call-update) | async-done | bytes 1572880 | tf_op jit(solution)/shard_map/reduce_scatter | solution.py:150
  584.1 113.5 %reduce-scatter.29.cloned.1.call-done = f32[512,768]{1,0:T(8,128)} async-done(((f32[2048,768]{1,0:T(8,128)}), f32[512,768]{1,0:T(8,128)}) %reduce-scatter.29.cloned.1.call-update) | async-done | bytes 1572880 | tf_op jit(solution)/shard_map/reduce_scatter | solution.py:150
  713.4 61.3 %all-gather.33.cloned.1.call-done = bf16[2048,768]{1,0:T(8,128)(2,1)} async-done(((bf16[512,768]{1,0:T(8,128)(2,1)}), bf16[2048,768]{1,0:T(8,128)(2,1)}) %all-gather.33.cloned.1.call-update) | async-done | bytes 3145744 | tf_op jit(solution)/shard_map/all_gather | solution.py:159
  774.7 7.4 fusion.506
  782.1 56.2 %all-gather.27.cloned.1.call-done = bf16[2048,768]{1,0:T(8,128)(2,1)} async-done(((bf16[512,768]{1,0:T(8,128)(2,1)}), bf16[2048,768]{1,0:T(8,128)(2,1)}) %all-gather.27.cloned.1.call-update) | async-done | bytes 3145744 | tf_op jit(solution)/shard_map/all_gather | solution.py:159
  838.3 17.3 %convert_reduce_fusion.1 = (f32[768]{0:T(1024)}, bf16[2048,768]{1,0:T(8,128)(2,1)S(1)}, f32[768]{0:T(1024)}, bf16[2048,768]{1,0:T(8,128)(2,1)}) fusion(f32[2048,768]{1,0:T(8,128)} %get-tuple-element.107, f32[2048,768]{1,0:T(8,128)} %get-tuple-element.228, f32[768]{0:T(1024)S(1)} %convert_element_type.300, f32[2048,768]{1,0:T(8,128)} %fusion.506, ...), kind=kOutput, calls=%fused_computation.17 | convolution fusion | flops 2469394944 | bytes 42083328 | tf_op jit(solution)/shard_map/rd,fd->rf/dot_general | solution.py:163
  857.2 4.5 fusion.501
  861.8 7.6 fusion.507
  869.5 101.9 %reduce-scatter.31.cloned.1.call-done = f32[512,768]{1,0:T(8,128)} async-done(((f32[2048,768]{1,0:T(8,128)}), f32[512,768]{1,0:T(8,128)}) %reduce-scatter.31.cloned.1.call-update) | async-done | bytes 1572880 | tf_op jit(solution)/shard_map/reduce_scatter | solution.py:168
  971.3 4.2 multiply_reduce_fusion.9
  975.5 109.8 %reduce-scatter.35.cloned.1.call-done = f32[512,768]{1,0:T(8,128)} async-done(((f32[2048,768]{1,0:T(8,128)}), f32[512,768]{1,0:T(8,128)}) %reduce-scatter.35.cloned.1.call-update) | async-done | bytes 1572880 | tf_op jit(solution)/shard_map/reduce_scatter | solution.py:168
  1085.4 4.5 fusion.464
  1097.7 59.5 %all-gather.35.cloned.1.call-done = bf16[2048,768]{1,0:T(8,128)(2,1)} async-done(((bf16[512,768]{1,0:T(8,128)(2,1)}), bf16[2048,768]{1,0:T(8,128)(2,1)}) %all-gather.35.cloned.1.call-update) | async-done | bytes 3145744 | tf_op jit(solution)/shard_map/all_gather | solution.py:174
  1164.1 7.6 fusion.325
  1171.7 7.0 fusion.322
  1178.8 5.2 fusion.331
  1184.0 5.2 fusion.328
  1190.8 5.2 fusion.319
  1196.0 5.2 fusion.316
  1204.7 5.6 fusion.337
  1210.3 5.2 fusion.334
  1223.0 4.1 bitcast_convert_fusion
  1233.8 5.2 fusion.301
  1239.0 5.3 fusion.298
  1245.8 5.3 fusion.307
  1251.1 5.4 fusion.304
  1258.1 5.2 fusion.295
  1263.3 5.3 fusion.292
  1272.1 5.4 fusion.313
  1277.4 5.2 fusion.310
  1290.1 4.1 bitcast_convert_fusion.1
  1306.2 4.1 fusion.20
  1310.3 3.9 add_bitcast_fusion
  1316.9 4.8 reshape.1305
  1324.2 65.8 %reduce-scatter.33.cloned.1.call-done = bf16[512,768]{1,0:T(8,128)(2,1)} async-done(((bf16[2048,768]{1,0:T(8,128)(2,1)}), bf16[512,768]{1,0:T(8,128)(2,1)}) %reduce-scatter.33.cloned.1.call-update) | async-done | bytes 786448 | tf_op jit(solution)/shard_map/reduce_scatter | solution.py:233
  1392.3 5.6 fusion.513
  1398.0 4.1 convolution_add_fusion
  1402.5 5.7 fusion.512
  1408.2 4.2 convolution_add_fusion.1
  1412.5 56.7 %all-gather.21.cloned.1.call-done = bf16[2048,768]{1,0:T(8,128)(2,1)} async-done(((bf16[512,768]{1,0:T(8,128)(2,1)}), bf16[2048,768]{1,0:T(8,128)(2,1)}) %all-gather.21.cloned.1.call-update) | async-done | bytes 3145744 | tf_op jit(solution)/shard_map/all_gather | solution.py:240
  1469.2 6.3 pad_maximum_fusion
  1477.3 9.8 all-reduce.1
  1489.7 13.7 all-reduce
  1505.1 38.8 %reduce-scatter.43.cloned.1.call-done = f32[96,576]{1,0:T(8,128)} async-done(((f32[768,576]{1,0:T(8,128)}), f32[96,576]{1,0:T(8,128)}) %reduce-scatter.43.cloned.1.call-update) | async-done | bytes 221200
  1545.8 51.5 %all-gather.31.cloned.1.call-done = bf16[2048,768]{1,0:T(8,128)(2,1)} async-done(((bf16[512,768]{1,0:T(8,128)(2,1)}), bf16[2048,768]{1,0:T(8,128)(2,1)}) %all-gather.31.cloned.1.call-update) | async-done | bytes 3145744 | tf_op jit(solution)/shard_map/all_gather | solution.py:241
  1597.3 6.3 pad_maximum_fusion.1
  1603.6 33.3 %reduce-scatter.39.cloned.1.call-done = f32[96,768]{1,0:T(8,128)} async-done(((f32[768,768]{1,0:T(8,128)}), f32[96,768]{1,0:T(8,128)}) %reduce-scatter.39.cloned.1.call-update) | async-done | bytes 294928 | tf_op jit(solution)/shard_map/reduce_scatter | solution.py:265
  (625 shorter events, 141.9 us)
Async XLA Ops:
  8.0 178.5 %reduce-scatter.27.cloned.1.call-start = ((), (), s32[]{:S(2)}) async-start(), calls=%async_computation.20 | async-start | bytes 7864320 | tf_op jit(solution)/shard_map/reduce_scatter | solution.py:141
  13.4 23.2 %slice-start = ((s8[6291456]{0:T(1024)(128)(4,1)}), s8[4194304]{0:T(1024)(128)(4,1)S(1)}, s32[]{:S(2)}) async-start(s8[6291456]{0:T(1024)(128)(4,1)} %bitcast.376), calls=%async_computation.40 | async-start | bytes 8388608
  28.3 8.3 copy-start.49
  28.3 8.3 slice-start.1
  36.6 5.5 copy-start.164
  36.6 6.2 copy-start.134
  44.0 19.5 %copy-start.52 = (pred[512,512]{0,1:T(8,128)(4,1)}, pred[512,512]{0,1:T(8,128)(4,1)S(1)}, u32[]{:S(2)}) copy-start(pred[512,512]{0,1:T(8,128)(4,1)S(1)} %compare_and_fusion.3) | copy-start | bytes 786436
  45.0 23.3 %copy-start.54 = (pred[512,512]{0,1:T(8,128)(4,1)}, pred[512,512]{0,1:T(8,128)(4,1)S(1)}, u32[]{:S(2)}) copy-start(pred[512,512]{0,1:T(8,128)(4,1)S(1)} %compare_and_fusion.2) | copy-start | bytes 786436
  46.2 19.7 %copy-start.55 = (pred[512,512]{0,1:T(8,128)(4,1)}, pred[512,512]{0,1:T(8,128)(4,1)S(1)}, u32[]{:S(2)}) copy-start(pred[512,512]{0,1:T(8,128)(4,1)S(1)} %compare_and_fusion.1) | copy-start | bytes 786436
  47.9 13.1 copy-start.53
  56.6 36.0 %copy-start.21 = (bf16[192,768]{0,1:T(8,128)(2,1)}, bf16[192,768]{0,1:T(8,128)(2,1)S(1)}, u32[]{:S(2)}) copy-start(bf16[192,768]{0,1:T(8,128)(2,1)S(1)} %all_gather.49) | copy-start | bytes 884740
  56.7 6.7 copy-start.71
  56.7 9.2 copy-start.72
  56.7 11.6 copy-start.74
  61.0 6.2 copy-start.62
  61.0 7.4 copy-start.77
  61.0 8.6 copy-start.64
  63.4 7.4 copy-start.102
  75.2 225.5 %reduce-scatter.23.cloned.1.call-start = ((), (), s32[]{:S(2)}) async-start(), calls=%async_computation.14 | async-start | bytes 7864320 | tf_op jit(solution)/shard_map/reduce_scatter | solution.py:141
  82.5 6.1 copy-start.59
  84.7 5.8 copy-start.67
  84.7 6.5 copy-start.68
  84.7 7.2 copy-start.69
  97.1 210.2 %all-gather.17.cloned.1.call-start = ((), (), s32[]{:S(2)}) async-start(), calls=%async_computation.16 | async-start | bytes 1327104 | tf_op jit(solution)/shard_map/all_gather | solution.py:81
  97.7 272.2 %all-gather.23.cloned.1.call-start = ((), (), s32[]{:S(2)}) async-start(), calls=%async_computation.21 | async-start | bytes 3932160 | tf_op jit(solution)/shard_map/all_gather | solution.py:146
  97.7 6.0 copy-start.189
  97.7 14.9 copy-start.188
  305.9 128.0 %all-gather.15.cloned.1.call-start = ((), (), s32[]{:S(2)}) async-start(), calls=%async_computation.15 | async-start | bytes 3932160 | tf_op jit(solution)/shard_map/all_gather | solution.py:146
  306.5 160.7 %all-gather.19.cloned.1.call-start = ((), (), s32[]{:S(2)}) async-start(), calls=%async_computation.17 | async-start | bytes 1327104 | tf_op jit(solution)/shard_map/all_gather | solution.py:82
  307.2 276.9 %reduce-scatter.25.cloned.1.call-start = ((), (), s32[]{:S(2)}) async-start(), calls=%async_computation.18 | async-start | bytes 7864320 | tf_op jit(solution)/shard_map/reduce_scatter | solution.py:150
  474.7 222.9 %reduce-scatter.29.cloned.1.call-start = ((), (), s32[]{:S(2)}) async-start(), calls=%async_computation.22 | async-start | bytes 7864320 | tf_op jit(solution)/shard_map/reduce_scatter | solution.py:150
  482.3 292.3 %all-gather.33.cloned.1.call-start = ((), (), s32[]{:S(2)}) async-start(), calls=%async_computation.29 | async-start | bytes 3932160 | tf_op jit(solution)/shard_map/all_gather | solution.py:159
  710.5 127.8 %all-gather.27.cloned.1.call-start = ((), (), s32[]{:S(2)}) async-start(), calls=%async_computation.24 | async-start | bytes 3932160 | tf_op jit(solution)/shard_map/all_gather | solution.py:159
  713.0 258.4 %reduce-scatter.31.cloned.1.call-start = ((), (), s32[]{:S(2)}) async-start(), calls=%async_computation.25 | async-start | bytes 7864320 | tf_op jit(solution)/shard_map/reduce_scatter | solution.py:168
  838.3 18.9 %copy-start.191 = (bf16[768,768]{1,0:T(8,128)(2,1)S(1)}, bf16[768,768]{1,0:T(8,128)(2,1)}, u32[]{:S(2)}) copy-start(bf16[768,768]{1,0:T(8,128)(2,1)} %all-gather.17.cloned.1.call-done) | copy-start | bytes 3538948
  861.8 223.6 %reduce-scatter.35.cloned.1.call-start = ((), (), s32[]{:S(2)}) async-start(), calls=%async_computation.30 | async-start | bytes 7864320 | tf_op jit(solution)/shard_map/reduce_scatter | solution.py:168
  869.4 287.9 %all-gather.35.cloned.1.call-start = ((), (), s32[]{:S(2)}) async-start(), calls=%async_computation.31 | async-start | bytes 3932160 | tf_op jit(solution)/shard_map/all_gather | solution.py:174
  1090.0 5.9 copy-start.125
  1090.0 5.9 copy-start.142
  1090.0 6.5 copy-start.18
  1092.3 65.0 %copy-start.22 = (bf16[192,768]{0,1:T(8,128)(2,1)S(1)}, bf16[192,768]{0,1:T(8,128)(2,1)}, u32[]{:S(2)}) copy-start(bf16[192,768]{0,1:T(8,128)(2,1)} %copy-done.21) | copy-start | bytes 884740
  1093.3 135.1 %all-gather.29.cloned.1.call-start = ((), (), s32[]{:S(2)}) async-start(), calls=%async_computation.26 | async-start | bytes 3932160 | tf_op jit(solution)/shard_map/all_gather | solution.py:174
  1097.5 63.7 %copy-start.65 = (bf16[512,192]{0,1:T(8,128)(2,1)S(1)}, bf16[512,192]{0,1:T(8,128)(2,1)}, u32[]{:S(2)}) copy-start(bf16[512,192]{0,1:T(8,128)(2,1)} %copy-done.64) | copy-start | bytes 589828
  1097.5 224.3 %reduce-scatter.37.cloned.1.call-start = ((), (), s32[]{:S(2)}) async-start(), calls=%async_computation.32 | async-start | bytes 3932160 | tf_op jit(solution)/shard_map/reduce_scatter | solution.py:233
  1227.1 162.9 %reduce-scatter.33.cloned.1.call-start = ((), (), s32[]{:S(2)}) async-start(), calls=%async_computation.27 | async-start | bytes 3932160 | tf_op jit(solution)/shard_map/reduce_scatter | solution.py:233
  1287.8 22.4 %copy-start.34 = (bf16[1,2048,192]{1,2,0:T(8,128)(2,1)}, bf16[1,2048,192]{1,2,0:T(8,128)(2,1)S(1)}, u32[]{:S(2)}) copy-start(bf16[1,2048,192]{1,2,0:T(8,128)(2,1)S(1)} %maximum_bitcast_fusion.2) | copy-start | bytes 2359300
  1294.4 118.1 %all-gather.25.cloned.1.call-start = ((), (), s32[]{:S(2)}) async-start(), calls=%async_computation.23 | async-start | bytes 3932160 | tf_op jit(solution)/shard_map/all_gather | solution.py:240
  1295.1 174.1 %all-gather.21.cloned.1.call-start = ((), (), s32[]{:S(2)}) async-start(), calls=%async_computation.19 | async-start | bytes 3932160 | tf_op jit(solution)/shard_map/all_gather | solution.py:240
  1295.9 179.7 %reduce-scatter.47.cloned.1.call-start = ((), (), s32[]{:S(2)}) async-start(), calls=%async_computation.38 | async-start | bytes 442368
  1297.2 179.2 %reduce-scatter.49.cloned.1.call-start = ((), (), s32[]{:S(2)}) async-start(), calls=%async_computation.39 | async-start | bytes 442368
  1298.3 205.2 %reduce-scatter.45.cloned.1.call-start = ((), (), s32[]{:S(2)}) async-start(), calls=%async_computation.37 | async-start | bytes 884736
  1305.9 238.1 %reduce-scatter.43.cloned.1.call-start = ((), (), s32[]{:S(2)}) async-start(), calls=%async_computation.36 | async-start | bytes 2211840
  1321.7 68.3 %copy-start.19 = (f32[512,768]{1,0:T(8,128)S(1)}, f32[512,768]{1,0:T(8,128)}, u32[]{:S(2)}) copy-start(f32[512,768]{1,0:T(8,128)} %get-tuple-element.95) | copy-start | bytes 4718596
  1321.7 224.1 %all-gather.37.cloned.1.call-start = ((), (), s32[]{:S(2)}) async-start(), calls=%async_computation.33 | async-start | bytes 3932160 | tf_op jit(solution)/shard_map/all_gather | solution.py:241
  1324.1 273.2 %all-gather.31.cloned.1.call-start = ((), (), s32[]{:S(2)}) async-start(), calls=%async_computation.28 | async-start | bytes 3932160 | tf_op jit(solution)/shard_map/all_gather | solution.py:241
  1392.2 5.7 copy-start.190
  1392.2 211.3 %reduce-scatter.41.cloned.1.call-start = ((), (), s32[]{:S(2)}) async-start(), calls=%async_computation.35 | async-start | bytes 2654208 | tf_op jit(solution)/shard_map/reduce_scatter | solution.py:266
  1392.3 5.7 copy-start.193
  1402.1 6.1 copy-start.43
  1402.1 234.7 %reduce-scatter.39.cloned.1.call-start = ((), (), s32[]{:S(2)}) async-start(), calls=%async_computation.34 | async-start | bytes 2654208 | tf_op jit(solution)/shard_map/reduce_scatter | solution.py:265
  1402.4 5.8 copy-start.44
  1469.2 17.9 %copy-start.35 = (bf16[1,2048,192]{1,2,0:T(8,128)(2,1)S(1)}, bf16[1,2048,192]{1,2,0:T(8,128)(2,1)}, u32[]{:S(2)}) copy-start(bf16[1,2048,192]{1,2,0:T(8,128)(2,1)} %copy-done.34) | copy-start | bytes 2359300
  1469.2 17.9 %copy-start.38 = (bf16[1,2048,192]{1,2,0:T(8,128)(2,1)S(1)}, bf16[1,2048,192]{1,2,0:T(8,128)(2,1)}, u32[]{:S(2)}) copy-start(bf16[1,2048,192]{1,2,0:T(8,128)(2,1)} %copy-done.36) | copy-start | bytes 2359300
  1469.2 17.9 %copy-start.41 = (bf16[1,2048,192]{1,2,0:T(8,128)(2,1)S(1)}, bf16[1,2048,192]{1,2,0:T(8,128)(2,1)}, u32[]{:S(2)}) copy-start(bf16[1,2048,192]{1,2,0:T(8,128)(2,1)} %copy-done.39) | copy-start | bytes 2359300
  (158 other events, 388.4 us)
Sparse Core Ops, SparseCore 0:
  75.4 111.1 reduce-scatter.26
  189.4 111.2 reduce-scatter.22
  710.6 64.0 all-gather.32
  776.1 62.1 all-gather.26
  861.9 109.3 reduce-scatter.30
  974.1 111.2 reduce-scatter.34
  1296.8 107.4 all-gather.24
  1405.9 63.2 all-gather.20
  1471.3 62.2 all-gather.36
  1535.1 62.1 all-gather.30
Sparse Core Ops, SparseCore 1:
  99.5 24.4 all-gather.16
  306.0 63.8 all-gather.22
  371.9 62.0 all-gather.14
  435.8 22.5 all-gather.18
  474.8 109.3 reduce-scatter.24
  586.4 111.1 reduce-scatter.28
  1093.4 63.8 all-gather.34
  1159.3 62.0 all-gather.28
  1227.2 58.9 reduce-scatter.36
  1294.5 95.5 reduce-scatter.32
  1392.9 32.3 reduce-scatter.46
  1428.3 33.9 reduce-scatter.48
  1465.3 34.9 reduce-scatter.44
  1503.7 40.1 reduce-scatter.42
  1548.2 42.3 reduce-scatter.40
  1594.5 42.3 reduce-scatter.38
where the time goes:
time: 1650 us; the launch traced here: 1640 us
  waiting for transfers between devices  1150 us (70%)
  matrix products  286 us (17%)
  other arithmetic  69.1 us (4%)
  blocking collectives  64.3 us (4%)
  local copies, waits for them, and re-layouts  53.1 us (3%)
  between operations  24.4 us (1%)
    reduce_scatter x2, waiting for transfers between devices, body(): lax.psum_scatter(back_partial, 'tensor', scatter_dimension=0, tiled=True)  212 us
    reduce_scatter x2, waiting for transfers between devices, body(): lax.psum_scatter(down_partial, 'tensor', scatter_dimension=0, tiled=True)  209 us
    reduce_scatter x2, waiting for transfers between devices, body(): lax.psum_scatter(attn_partial, 'tensor', scatter_dimension=0, tiled=True)  180 us
    all_gather x2, waiting for transfers between devices, body(): first_low = lax.all_gather(first_share, 'tensor', axis=0, tiled=True)  119 us
    all_gather x2, waiting for transfers between devices, body(): second_low = lax.all_gather(second_share, 'tensor', axis=0, tiled=True)  117 us
    reduce_scatter x2, waiting for transfers between devices, body(): lax.psum_scatter(token_partial.astype(jnp.bfloat16), 'tensor', scatter_di...  65.9 us
    all_gather x2, waiting for transfers between devices, body(): hidden_low = lax.all_gather(hidden_share, 'tensor', axis=0, tiled=True)  59.6 us
    all_gather x2, waiting for transfers between devices, body(): lax.all_gather(result_low, 'tensor', axis=0, tiled=True)  56.7 us
  transfers between devices with their start and end apart: 26, of which 16 were waited for; matrix products, arithmetic and copies ran while one was open for 19% of the time, Pallas kernels for 0%

commit v1 on v0

v1 whole, which is shorter than its diff:
```python
import jax
import jax.numpy as jnp
from jax import lax
from jax.sharding import PartitionSpec as P

HEAD_DIM = 64


EPSILON = 1e-12


def token_masks(bucket_id, item_lengths, item_count, slot_count):
    position = jnp.arange(slot_count, dtype=jnp.int32)
    item_size = jnp.where(bucket_id == 1, slot_count, slot_count // 4).astype(jnp.int32)
    item_index = position // item_size
    within = position % item_size
    picked = item_index[:, None] == jnp.arange(4, dtype=jnp.int32)[None, :]
    length_of = jnp.sum(jnp.where(picked, item_lengths[None, :], 0), axis=1)
    is_live = (item_index < item_count) & (within < length_of)
    keymask = (item_index[:, None] == item_index[None, :]) & is_live[None, :]
    return (is_live, keymask)


def gelu_exact(argument):
    return jax.nn.gelu(argument, approximate=False)


def norm_forward(hidden, gain_row, shift_row):
    center = hidden - jnp.mean(hidden, axis=-1, keepdims=True)
    inverse = lax.rsqrt(jnp.mean(center * center, axis=-1, keepdims=True) + EPSILON)
    normed = center * inverse
    return (normed * gain_row + shift_row, normed, inverse)


def norm_backward(grad_rows, normed, inverse, gain_row):
    grad_normed = grad_rows * gain_row
    grad_input = inverse * (
        grad_normed
        - jnp.mean(grad_normed, axis=-1, keepdims=True)
        - normed * jnp.mean(grad_normed * normed, axis=-1, keepdims=True)
    )
    return (grad_input, jnp.sum(grad_rows * normed, axis=0), jnp.sum(grad_rows, axis=0))


def block_scores(query_rows, key_rows, keymask):
    slot_count = query_rows.shape[0]
    query_heads = query_rows.reshape(slot_count, -1, HEAD_DIM)
    key_heads = key_rows.reshape(slot_count, -1, HEAD_DIM)
    scores = jnp.einsum(
        "qhd,khd->hqk", query_heads, key_heads, preferred_element_type=jnp.float32
    ) * HEAD_DIM ** (-0.5)
    return jnp.where(keymask[None], scores, -10000.0)


def add_tuples(earlier, latest):
    return tuple((first_term + second_term for first_term, second_term in zip(earlier, latest)))


def packed_shards(w_qkv, w_out, w_in, w_down):
    head_slab = jnp.concatenate([w_qkv[0], w_qkv[1], w_qkv[2], w_out.T], axis=1)
    return (head_slab, w_in, w_down.T)


def body(
    inputs,
    cotangent,
    bucket,
    lengths,
    counts,
    w_qkv,
    w_out,
    w_in,
    w_down,
    head_bias,
    ffn_bias,
    norm_gains,
    row_biases,
):
    micro_count = inputs.shape[0]
    blocks_all = bucket.shape[1]
    slot_count = inputs.shape[1] // blocks_all
    score_scale = HEAD_DIM ** (-0.5)
    parts = lax.axis_size("tensor")
    rank = lax.axis_index("tensor")
    width = inputs.shape[2]
    head_cols = w_out.shape[0]
    share_blocks = blocks_all // parts
    share_count = share_blocks * slot_count
    share_start = rank * share_count

    slabs = packed_shards(w_qkv, w_out, w_in, w_down)
    full = [lax.all_gather(s, ("tensor", "dp"), axis=0, tiled=True).reshape(parts, width, s.shape[1]) for s in slabs]
    mat_head, mat_in, mat_down = full
    mat_in = mat_in.transpose(1, 0, 2).reshape(width, -1)
    mat_down = mat_down.transpose(1, 0, 2).reshape(width, -1)
    split = mat_head.reshape(parts, width, 4, head_cols).transpose(2, 1, 0, 3).reshape(4, width, width)
    gain_rows = lax.all_gather(norm_gains, "dp", axis=1, tiled=True).astype(jnp.float32)
    shifts = lax.all_gather(row_biases, "dp", axis=1, tiled=True).astype(jnp.float32)
    column_bias = lax.all_gather(head_bias, "tensor", axis=1, tiled=True).astype(jnp.float32)
    hidden_bias = lax.all_gather(ffn_bias, "tensor", axis=0, tiled=True).astype(jnp.float32)

    results = []
    input_grads = []
    kept = None
    for micro_index in range(micro_count):
        tokens = lax.dynamic_slice_in_dim(inputs[micro_index], share_start, share_count, 0)
        cot_rows = lax.dynamic_slice_in_dim(cotangent[micro_index], share_start, share_count, 0)
        bucket_rows = lax.dynamic_slice_in_dim(bucket[micro_index], rank * share_blocks, share_blocks, 0)
        length_rows = lax.dynamic_slice_in_dim(lengths[micro_index], rank * share_blocks, share_blocks, 0)
        count_rows = lax.dynamic_slice_in_dim(counts[micro_index], rank * share_blocks, share_blocks, 0)
        query_rows = (jnp.dot(tokens, split[0], preferred_element_type=jnp.float32) + column_bias[0]).astype(jnp.bfloat16)
        key_rows = jnp.dot(tokens, split[1], preferred_element_type=jnp.float32).astype(jnp.bfloat16)
        values = (jnp.dot(tokens, split[2], preferred_element_type=jnp.float32) + column_bias[1]).astype(jnp.bfloat16)
        live_parts, mask_parts, prob_parts, context_parts = ([], [], [], [])
        for block_index in range(share_blocks):
            rows = slice(block_index * slot_count, (block_index + 1) * slot_count)
            is_live, keymask = token_masks(
                bucket_rows[block_index], length_rows[block_index], count_rows[block_index], slot_count
            )
            scores = block_scores(query_rows[rows], key_rows[rows], keymask)
            row_peak = jnp.max(scores, axis=-1, keepdims=True)
            exp_scores = jnp.exp(scores - row_peak)
            totals = jnp.sum(exp_scores, axis=-1, keepdims=True)
            attn_probs = (exp_scores / totals).astype(jnp.bfloat16)
            value_heads = values[rows].reshape(slot_count, -1, HEAD_DIM)
            context = jnp.einsum("hqk,khd->qhd", attn_probs, value_heads, preferred_element_type=jnp.float32)
            context_parts.append(context.reshape(slot_count, -1).astype(jnp.bfloat16))
            live_parts.append(is_live)
            mask_parts.append(keymask)
            prob_parts.append(attn_probs)
        context_all = jnp.concatenate(context_parts, axis=0)
        live_share = jnp.concatenate(live_parts, axis=0).astype(jnp.float32)
        attention = jnp.einsum("rc,dc->rd", context_all, split[3], preferred_element_type=jnp.float32)
        first_norm, normed_one, inverse_one = norm_forward(
            tokens.astype(jnp.float32) + attention + shifts[0], gain_rows[0], shifts[1]
        )
        first_low = first_norm.astype(jnp.bfloat16)
        upward = jnp.dot(first_low, mat_in, preferred_element_type=jnp.float32) + hidden_bias
        activated = gelu_exact(upward).astype(jnp.bfloat16)
        down_sum = jnp.einsum("rf,df->rd", activated, mat_down, preferred_element_type=jnp.float32)
        result, normed_two, inverse_two = norm_forward(
            first_norm + down_sum + shifts[2], gain_rows[1], shifts[3]
        )
        results.append(lax.all_gather(result.astype(jnp.bfloat16), "tensor", axis=0, tiled=True))
        grad_out = cot_rows.astype(jnp.float32) * live_share[:, None]
        grad_second, gain_two, shift_two = norm_backward(grad_out, normed_two, inverse_two, gain_rows[1])
        second_low = grad_second.astype(jnp.bfloat16)
        grad_down_w = jnp.einsum("rd,rf->df", second_low, activated, preferred_element_type=jnp.float32)
        grad_act = jnp.einsum("rd,df->rf", second_low, mat_down, preferred_element_type=jnp.float32)
        pullback = jax.vjp(gelu_exact, upward)[1]
        grad_up = pullback(grad_act)[0].astype(jnp.bfloat16)
        grad_in_w = jnp.einsum("rd,rf->df", first_low, grad_up, preferred_element_type=jnp.float32)
        back_total = jnp.einsum("rf,df->rd", grad_up, mat_in, preferred_element_type=jnp.float32)
        grad_first = grad_second + back_total
        grad_hidden, gain_one, shift_one = norm_backward(grad_first, normed_one, inverse_one, gain_rows[0])
        hidden_low = grad_hidden.astype(jnp.bfloat16)
        grad_out_w = jnp.einsum("rd,rc->dc", hidden_low, context_all, preferred_element_type=jnp.float32)
        grad_context = jnp.dot(hidden_low, split[3], preferred_element_type=jnp.float32).astype(jnp.bfloat16)
        query_parts, key_parts, value_parts = ([], [], [])
        for block_index in range(share_blocks):
            rows = slice(block_index * slot_count, (block_index + 1) * slot_count)
            attn_probs = prob_parts[block_index].astype(jnp.float32)
            context_heads = grad_context[rows].reshape(slot_count, -1, HEAD_DIM)
            value_heads = values[rows].reshape(slot_count, -1, HEAD_DIM)
            query_heads = query_rows[rows].reshape(slot_count, -1, HEAD_DIM)
            key_heads = key_rows[rows].reshape(slot_count, -1, HEAD_DIM)
            grad_values = jnp.einsum("hqk,qhd->khd", prob_parts[block_index], context_heads, preferred_element_type=jnp.float32)
            grad_probs = jnp.einsum("qhd,khd->hqk", context_heads, value_heads, preferred_element_type=jnp.float32)
            row_inner = jnp.sum(attn_probs * grad_probs, axis=-1, keepdims=True)
            grad_scores = jnp.where(
                mask_parts[block_index][None], attn_probs * (grad_probs - row_inner), 0.0
            ).astype(jnp.bfloat16)
            grad_query = jnp.einsum("hqk,khd->qhd", grad_scores, key_heads, preferred_element_type=jnp.float32) * score_scale
            grad_keys = jnp.einsum("hqk,qhd->khd", grad_scores, query_heads, preferred_element_type=jnp.float32) * score_scale
            query_parts.append(grad_query.reshape(slot_count, -1))
            key_parts.append(grad_keys.reshape(slot_count, -1))
            value_parts.append(grad_values.reshape(slot_count, -1))
        grad_qkv = jnp.stack(
            [jnp.concatenate(query_parts, axis=0), jnp.concatenate(key_parts, axis=0), jnp.concatenate(value_parts, axis=0)]
        ).astype(jnp.bfloat16)
        grad_qkv_w = jnp.einsum("rd,trc->tdc", tokens, grad_qkv, preferred_element_type=jnp.float32)
        token_total = jnp.einsum("trc,tdc->rd", grad_qkv, split[:3], preferred_element_type=jnp.float32)
        grad_tokens = (grad_hidden + token_total).astype(jnp.bfloat16)
        input_grads.append(lax.all_gather(grad_tokens, "tensor", axis=0, tiled=True))
        grad_qkv_wide = grad_qkv.astype(jnp.float32)
        now = (
            grad_qkv_w,
            grad_out_w,
            grad_in_w,
            grad_down_w,
            jnp.stack([gain_one, gain_two]),
            jnp.stack([jnp.sum(grad_hidden, axis=0), shift_one, jnp.sum(grad_second, axis=0), shift_two]),
            jnp.stack([jnp.sum(grad_qkv_wide[0], axis=0), jnp.sum(grad_qkv_wide[2], axis=0)]),
            jnp.sum(grad_up.astype(jnp.float32), axis=0),
        )
        kept = now if kept is None else add_tuples(kept, now)
    both = ("tensor", "dp")
    heads = jnp.concatenate([kept[0], kept[1][None]], axis=0)
    heads = heads.reshape(4, width, parts, head_cols).transpose(2, 1, 0, 3).reshape(parts * width, 4 * head_cols)
    ins = kept[2].reshape(width, parts, -1).transpose(1, 0, 2).reshape(parts * width, -1)
    downs = kept[3].reshape(width, parts, -1).transpose(1, 0, 2).reshape(parts * width, -1)
    heads, ins, downs = [
        lax.psum_scatter(v.astype(jnp.bfloat16), both, scatter_dimension=0, tiled=True).astype(jnp.float32)
        for v in (heads, ins, downs)
    ]
    gains_sum = lax.psum_scatter(lax.psum(kept[4], "tensor"), "dp", scatter_dimension=1, tiled=True)
    shifts_sum = lax.psum_scatter(lax.psum(kept[5], "tensor"), "dp", scatter_dimension=1, tiled=True)
    head_sum = lax.psum_scatter(lax.psum(kept[6], "dp"), "tensor", scatter_dimension=1, tiled=True)
    ffn_sum = lax.psum_scatter(lax.psum(kept[7], "dp"), "tensor", scatter_dimension=0, tiled=True)
    heads = heads.reshape(-1, 4, head_cols).transpose(1, 0, 2)
    return (
        jnp.stack(results),
        jnp.stack(input_grads),
        heads[:3],
        heads[3].T,
        ins,
        downs.T,
        head_sum,
        ffn_sum,
        gains_sum,
        shifts_sum,
    )


def solution(mesh):
    in_specs = (
        P(None, "dp", None),
        P(None, "dp", None),
        P(None, "dp"),
        P(None, "dp", None),
        P(None, "dp"),
        P(None, "dp", "tensor"),
        P("tensor", "dp"),
        P("dp", "tensor"),
        P("tensor", "dp"),
        P(None, "tensor"),
        P("tensor"),
        P(None, "dp"),
        P(None, "dp"),
    )
    out_specs = (
        P(None, "dp", None),
        P(None, "dp", None),
        P(None, "dp", "tensor"),
        P("tensor", "dp"),
        P("dp", "tensor"),
        P("tensor", "dp"),
        P(None, "tensor"),
        P("tensor"),
        P(None, "dp"),
        P(None, "dp"),
    )
    return jax.shard_map(body, mesh=mesh, in_specs=in_specs, out_specs=out_specs, check_vma=False)
```

time: 1650 us -> 1140 us (0.69)
  waiting for transfers between devices: 1150 us -> 616 us
  local copies, waits for them, and re-layouts: 53.1 us -> 137 us
  matrix products: 286 us -> 241 us
  other arithmetic: 69.1 us -> 50.3 us
    reduce_scatter x10 -> x2, waiting for transfers between devices: 699 us -> 220 us  [body(): lax.psum_scatter(v.astype(jnp.bfloat16), both, scatter_dimension=0, tiled...]
    all_gather x12 -> x7, waiting for transfers between devices: 404 us -> 287 us  [the longest x2 121 us: body(): lax.all_gather(grad_tokens, 'tensor', axis=0, tiled=True)]
    unnamed x30 -> x17, waiting for transfers between devices: 42.3 us -> 109 us
    convert_element_type x2 -> x15, local copies, waits for them, and re-layouts: 0.16 us -> 39.9 us  [the longest x4 29.9 us: body(): v.astype(jnp.bfloat16)]
    dot_general x32 -> x22, matrix products: 105 us -> 70.3 us  [the longest x2 18.3 us: body(): jnp.einsum('rd,df->rf', second_low, mat_down, preferred_element_type=jnp....]
    another operation x0 -> x11, local copies, waits for them, and re-layouts: none -> 21.2 us  [the longest x6 11.4 us: body(): jnp.stack([jnp.concatenate(query_parts, axis=0), jnp.concatenate(key_part...]
    unnamed x0 -> x1, blocking collectives: none -> 19.7 us
    dot_general x8 -> x2, matrix products: 44.7 us -> 29.7 us  [body(): jnp.einsum('hqk,khd->qhd', grad_scores, key_heads, preferred_element_type...]
  transfers between devices with their start and end apart: 26 -> 13, of which waited for: 16 -> 10; matrix products, arithmetic and copies ran while one was open for 19% -> 16% of each run, Pallas kernels for 0% -> 0%
where the time goes in v1:
time: 1140 us
  waiting for transfers between devices  616 us (54%)
  matrix products  241 us (21%)
  local copies, waits for them, and re-layouts  137 us (12%)
  blocking collectives  76.6 us (7%)
  other arithmetic  50.3 us (4%)
  between operations  17.4 us (2%)
    reduce_scatter x2, waiting for transfers between devices, body(): lax.psum_scatter(v.astype(jnp.bfloat16), both, scatter_dimension=0, tiled...  220 us
    all_gather x2, waiting for transfers between devices, body(): lax.all_gather(grad_tokens, 'tensor', axis=0, tiled=True)  121 us
    unnamed x17, waiting for transfers between devices  109 us
    all_gather x3, waiting for transfers between devices, body(): lax.all_gather(s, ('tensor', 'dp'), axis=0, tiled=True)  95.7 us
    all_gather x2, waiting for transfers between devices, body(): lax.all_gather(result.astype(jnp.bfloat16), 'tensor', axis=0, tiled=True)  70.1 us
    dot_general x2, matrix products, body(): jnp.dot(first_low, mat_in, preferred_element_type=jnp.float32) + hidden_bias  44.1 us
    dot_general x2, matrix products, body(): jnp.einsum('hqk,qhd->khd', grad_scores, query_heads, preferred_element_ty...  34 us
    convert_element_type x4, local copies, waits for them, and re-layouts, body(): v.astype(jnp.bfloat16)  29.9 us
  transfers between devices with their start and end apart: 13, of which 10 were waited for; matrix products, arithmetic and copies ran while one was open for 16% of the time, Pallas kernels for 0%

profile of v1, /device:TPU:0, one launch (start us, length us, event | category | flops | bytes accessed | tf_op | source)
XLA Modules:
  0.0 1138.8 jit_solution(6484134725794736665)
XLA Ops:
  15.2 12.8 %all-gather = bf16[4,192,2]{1,2,0:T(2,128)(2,1)S(1)} all-gather(bf16[1,192,2]{1,2,0:T(2,128)(2,1)} %bitcast.304), channel_id=1, replica_groups=mesh['dp'=8,'tensor'=4] {'tensor'}, dimensions={0}, use_global_device_ids=true | all-gather | bytes 3840 | tf_op jit(solution)/shard_map/all_gather | solution.py:99
  28.2 8.8 all-gather.2
  37.1 8.8 all-gather.1
  46.0 13.0 %all-gather.3 = bf16[4,1,768]{2,1,0:T(2,128)(2,1)S(1)} all-gather(bf16[1,1,768]{2,1,0:T(2,128)(2,1)S(1)} %reshape.439), channel_id=1, replica_groups=mesh['dp'=8,'tensor'=4] {'tensor'}, dimensions={0}, use_global_device_ids=true | all-gather | bytes 7680 | tf_op jit(solution)/shard_map/all_gather | solution.py:100
  67.2 6.5 fusion.145
  73.7 3.1 fusion.144
  77.3 6.9 copy.242
  84.2 59.1 %all-gather.12.cloned.1.call-done = bf16[3072,768]{1,0:T(8,128)(2,1)} async-done(((bf16[96,768]{1,0:T(8,128)(2,1)}), bf16[3072,768]{1,0:T(8,128)(2,1)}) %all-gather.12.cloned.1.call-update) | async-done | bytes 4718608 | tf_op jit(solution)/shard_map/all_gather | solution.py:92
  143.3 6.6 copy.230
  149.9 9.8 reshape_reshape.3
  159.7 3.3 fusion.146
  172.6 36.0 %all-gather.16.cloned.1.call-done = bf16[3072,768]{1,0:T(8,128)(2,1)} async-done(((bf16[96,768]{1,0:T(8,128)(2,1)}), bf16[3072,768]{1,0:T(8,128)(2,1)}) %all-gather.16.cloned.1.call-update) | async-done | bytes 4718608 | tf_op jit(solution)/shard_map/all_gather | solution.py:92
  208.7 6.6 copy.243
  225.7 8.0 fusion.151
  233.8 6.4 divide_convert_fusion.1
  240.2 2.9 convolution_convert_fusion.7
  246.8 7.5 fusion.154
  254.3 6.4 divide_convert_fusion
  260.8 2.9 convolution_convert_fusion.6
  266.6 7.3 fusion.128
  273.9 36.8 %multiply_convert_fusion.1 = (bf16[512,3072]{1,0:T(8,128)(2,1)S(1)}, f32[512,3072]{1,0:T(8,128)}, bf16[512,3072]{1,0:T(8,128)(2,1)S(1)}, f32[512,3072]{1,0:T(8,128)}, f32[512,3072]{1,0:T(8,128)}) fusion(f32[3072]{0:T(1024)S(1)} %bitcast.301, f32[512,3072]{1,0:T(8,128)} %fusion.128, bf16[768,3072]{0,1:T(8,128)(2,1)S(1)} %bitcast.246, ...), kind=kOutput, calls=%fused_computation.48 | convolution fusion | flops 2625503232 | bytes 37771264 | tf_op jit(solution)/shard_map/dot_general | solution.py:138
  310.8 2.8 fusion.156
  313.9 2.8 fusion.157
  321.4 9.3 convert_reduce_fusion.1
  330.7 5.0 multiply_reduce_fusion.1
  335.7 9.0 convert_reduce_fusion
  344.7 6.3 fusion.137
  353.3 5.8 convolution_convert_fusion.5
  359.1 6.4 fusion.158
  365.5 15.0 %multiply_convert_fusion.5 = bf16[12,64,512]{2,1,0:T(8,128)(2,1)} fusion(bf16[512,12,64]{0,2,1:T(8,128)(2,1)S(1)} %bitcast.285, bf16[12,512,512]{1,2,0:T(8,128)(2,1)} %copy-done.1, f32[12,512,512]{1,2,0:T(8,128)} %fusion.158, pred[512,512]{0,1:T(8,128)(4,1)S(1)} %copy-done.51), kind=kOutput, calls=%fused_computation.114 | convolution fusion | flops 425466368 | bytes 20709376 | tf_op jit(solution)/shard_map/hqk,khd->qhd/dot_general | solution.py:173
  380.6 17.1 %multiply_convert_fusion.4 = bf16[12,64,512]{2,1,0:T(8,128)(2,1)} fusion(bf16[512,12,64]{0,2,1:T(8,128)(2,1)} %bitcast.287, bf16[12,512,512]{1,2,0:T(8,128)(2,1)} %copy-done.1, f32[12,512,512]{1,2,0:T(8,128)} %fusion.158, pred[512,512]{0,1:T(8,128)(4,1)S(1)} %copy-done.51), kind=kOutput, calls=%fused_computation.113 | convolution fusion | flops 425466368 | bytes 20709376 | tf_op jit(solution)/shard_map/hqk,qhd->khd/dot_general | solution.py:174
  401.9 5.7 convolution_convert_fusion.4
  407.7 6.4 fusion.159
  414.1 14.7 %multiply_convert_fusion.3 = bf16[12,64,512]{2,1,0:T(8,128)(2,1)} fusion(bf16[512,12,64]{0,2,1:T(8,128)(2,1)S(1)} %bitcast.281, bf16[12,512,512]{1,2,0:T(8,128)(2,1)} %copy-done, f32[12,512,512]{1,2,0:T(8,128)} %fusion.159, pred[512,512]{0,1:T(8,128)(4,1)S(1)} %copy-done.49), kind=kOutput, calls=%fused_computation.110 | convolution fusion | flops 425466368 | bytes 20709376 | tf_op jit(solution)/shard_map/hqk,khd->qhd/dot_general | solution.py:173
  428.8 16.9 %multiply_convert_fusion.2 = bf16[12,64,512]{2,1,0:T(8,128)(2,1)} fusion(bf16[512,12,64]{0,2,1:T(8,128)(2,1)} %bitcast.282, bf16[12,512,512]{1,2,0:T(8,128)(2,1)} %copy-done, f32[12,512,512]{1,2,0:T(8,128)} %fusion.159, pred[512,512]{0,1:T(8,128)(4,1)S(1)} %copy-done.49), kind=kOutput, calls=%fused_computation.109 | convolution fusion | flops 425466368 | bytes 20709376 | tf_op jit(solution)/shard_map/hqk,qhd->khd/dot_general | solution.py:174
  448.8 2.6 copy.253
  465.9 3.2 slice.167
  472.0 3.0 fusion.55
  475.0 5.9 fusion.54
  485.4 3.4 fusion.63
  488.8 3.4 add_convert_fusion.2
  492.2 2.7 copy.267
  494.9 3.6 pad_maximum_fusion.2
  498.6 3.2 copy.292
  501.8 6.6 copy.284
  508.6 5.4 fusion.130
  514.0 4.8 add_convert_fusion.1
  518.8 9.8 convert_element_type.249
  528.5 5.1 copy.269
  535.0 4.7 fusion.89
  539.7 4.3 add_convert_fusion
  544.0 9.8 convert_element_type.254
  553.9 5.2 copy.270
  563.7 19.7 %all-reduce.2 = (f32[3072]{0:T(1024)S(1)}, f32[2,96]{1,0:T(2,128)}, f32[4,96]{1,0:T(4,128)}) all-reduce(f32[3072]{0:T(1024)S(1)} %add.334, f32[2,96]{1,0:T(2,128)S(1)} %copy.289, f32[4,96]{1,0:T(4,128)S(1)} %copy.291), channel_id=6, replica_groups=mesh['dp'=8,'tensor'=4] {'tensor'}, use_global_device_ids=true, to_apply=%region_36.37.clone | all-reduce | flops 3648 | bytes 29184
  583.5 13.5 %all-reduce.1 = (f32[2,192]{1,0:T(2,128)}, f32[768]{0:T(1024)}) all-reduce(f32[2,192]{1,0:T(2,128)S(1)} %copy.287, f32[768]{0:T(1024)S(1)} %dynamic-slice.11), channel_id=1, replica_groups=mesh['dp'=8,'tensor'=4] {'dp'}, use_global_device_ids=true, to_apply=%region_31.32 | all-reduce | flops 1152 | bytes 9216 | tf_op jit(solution)/shard_map/psum | solution.py:208
  596.9 6.3 all-gather.20.cloned.1.call-done
  603.2 63.8 %all-gather.18.cloned.1.call-done = bf16[2048,768]{1,0:T(8,128)(2,1)} async-done(((bf16[512,768]{1,0:T(8,128)(2,1)}), bf16[2048,768]{1,0:T(8,128)(2,1)}) %all-gather.18.cloned.1.call-update) | async-done | bytes 3145744 | tf_op jit(solution)/shard_map/all_gather | solution.py:144
  667.0 6.1 pad_maximum_fusion
  673.1 57.7 %all-gather.22.cloned.1.call-done = bf16[2048,768]{1,0:T(8,128)(2,1)} async-done(((bf16[512,768]{1,0:T(8,128)(2,1)}), bf16[2048,768]{1,0:T(8,128)(2,1)}) %all-gather.22.cloned.1.call-update) | async-done | bytes 3145744 | tf_op jit(solution)/shard_map/all_gather | solution.py:184
  730.8 63.7 %all-gather.24.cloned.1.call-done = bf16[2048,768]{1,0:T(8,128)(2,1)} async-done(((bf16[512,768]{1,0:T(8,128)(2,1)}), bf16[2048,768]{1,0:T(8,128)(2,1)}) %all-gather.24.cloned.1.call-update) | async-done | bytes 3145744 | tf_op jit(solution)/shard_map/all_gather | solution.py:184
  794.5 6.1 pad_maximum_fusion.1
  800.6 105.9 %reduce-scatter.19.cloned.1.call-done = bf16[96,768]{1,0:T(8,128)(2,1)} async-done(((bf16[3072,768]{1,0:T(8,128)(2,1)}), bf16[96,768]{1,0:T(8,128)(2,1)}) %reduce-scatter.19.cloned.1.call-update) | async-done | bytes 147472
  908.6 109.4 %reduce-scatter.15.cloned.1.call-done = bf16[96,768]{1,0:T(8,128)(2,1)} async-done(((bf16[3072,768]{1,0:T(8,128)(2,1)}), bf16[96,768]{1,0:T(8,128)(2,1)}) %reduce-scatter.15.cloned.1.call-update) | async-done | bytes 147472 | tf_op jit(solution)/shard_map/reduce_scatter | solution.py:203
  1020.3 110.2 %reduce-scatter.17.cloned.1.call-done = bf16[96,768]{1,0:T(8,128)(2,1)} async-done(((bf16[3072,768]{1,0:T(8,128)(2,1)}), bf16[96,768]{1,0:T(8,128)(2,1)}) %reduce-scatter.17.cloned.1.call-update) | async-done | bytes 147472 | tf_op jit(solution)/shard_map/reduce_scatter | solution.py:203
  (289 shorter events, 89.5 us)
Async XLA Ops:
  7.2 70.2 %all-gather.14.cloned.1.call-start = ((), (), s32[]{:S(2)}) async-start(), calls=%async_computation.7 | async-start | bytes 4866048 | tf_op jit(solution)/shard_map/all_gather | solution.py:92
  7.9 135.4 %all-gather.12.cloned.1.call-start = ((), (), s32[]{:S(2)}) async-start(), calls=%async_computation.6 | async-start | bytes 4866048 | tf_op jit(solution)/shard_map/all_gather | solution.py:92
  10.5 198.2 %all-gather.16.cloned.1.call-start = ((), (), s32[]{:S(2)}) async-start(), calls=%async_computation.8 | async-start | bytes 4866048 | tf_op jit(solution)/shard_map/all_gather | solution.py:92
  11.2 549.7 %reduce-scatter.23.cloned.1.call-start = ((), (), s32[]{:S(2)}) async-start(), calls=%async_computation.17 | async-start | bytes 442368
  66.3 7.4 slice-start
  67.2 6.5 slice-start.1
  219.1 6.7 copy-start.45
  219.1 6.6 copy-start.50
  222.0 11.8 %copy-start.47 = (bf16[512,768]{0,1:T(8,128)(2,1)}, bf16[512,768]{0,1:T(8,128)(2,1)S(1)}, u32[]{:S(2)}) copy-start(bf16[512,768]{0,1:T(8,128)(2,1)S(1)} %copy.235) | copy-start | bytes 2359300
  240.2 3.0 copy-start.1
  240.2 3.0 copy-start.38
  240.2 3.0 copy-start.59
  243.2 2.7 copy-start.6
  243.2 3.6 copy-start.42
  243.2 3.6 copy-start.44
  243.2 3.6 copy-start.48
  260.8 3.0 copy-start
  260.8 3.0 copy-start.39
  263.8 2.7 copy-start.8
  263.8 2.7 copy-start.57
  263.8 10.1 slice-start.2
  266.2 78.5 %copy-start.10 = (f32[512,768]{1,0:T(8,128)}, f32[512,768]{1,0:T(8,128)S(1)}, u32[]{:S(2)}) copy-start(f32[512,768]{1,0:T(8,128)S(1)} %get-tuple-element.158) | copy-start | bytes 4718596
  266.5 7.4 slice-start.3
  266.5 7.4 copy-start.35
  266.5 44.2 %slice-start.4 = ((s8[4718592]{0:T(1024)(128)(4,1)}), s8[4194304]{0:T(1024)(128)(4,1)S(1)}, s32[]{:S(2)}) async-start(s8[4718592]{0:T(1024)(128)(4,1)} %bitcast.251), calls=%async_computation.23 | async-start | bytes 8388608
  273.9 36.8 %slice-start.5 = ((s8[4718592]{0:T(1024)(128)(4,1)}), s8[524288]{0:T(1024)(128)(4,1)S(1)}, s32[]{:S(2)}) async-start(s8[4718592]{0:T(1024)(128)(4,1)} %bitcast.251), calls=%async_computation.24 | async-start | bytes 1048576
  273.9 36.8 %copy-start.58 = (f32[768]{0:T(1024)S(1)}, f32[768]{0:T(1024)}, u32[]{:S(2)}) copy-start(f32[768]{0:T(1024)} %get-tuple-element.91) | copy-start | bytes 9220
  310.7 2.8 copy-start.18
  310.7 3.2 copy-start.31
  313.9 3.2 copy-start.4
  313.9 3.2 copy-start.5
  313.9 3.2 copy-start.52
  313.9 3.2 copy-start.53
  313.9 3.2 copy-start.54
  321.4 9.3 copy-start.13
  344.7 7.5 copy-start.40
  353.3 5.8 copy-start.3
  359.1 6.4 copy-start.46
  359.1 6.4 copy-start.51
  380.5 17.1 %copy-start.11 = (f32[512,768]{1,0:T(8,128)S(1)}, f32[512,768]{1,0:T(8,128)}, u32[]{:S(2)}) copy-start(f32[512,768]{1,0:T(8,128)} %copy-done.10) | copy-start | bytes 4718596
  397.6 3.2 copy-start.41
  401.9 5.8 copy-start.2
  407.7 6.4 copy-start.43
  407.7 6.4 copy-start.49
  428.7 18.0 %copy-start.33 = (bf16[12,64,512]{2,1,0:T(8,128)(2,1)S(1)}, bf16[12,64,512]{2,1,0:T(8,128)(2,1)}, u32[]{:S(2)}) copy-start(bf16[12,64,512]{2,1,0:T(8,128)(2,1)} %convolution_convert_fusion.4) | copy-start | bytes 2359300
  446.7 115.1 %reduce-scatter.21.cloned.1.call-start = ((), (), s32[]{:S(2)}) async-start(), calls=%async_computation.16 | async-start | bytes 491520
  447.1 28.0 %copy-start.19 = (bf16[1,512,768]{2,1,0:T(8,128)(2,1)}, bf16[1,512,768]{2,1,0:T(8,128)(2,1)S(1)}, u32[]{:S(2)}) copy-start(bf16[1,512,768]{2,1,0:T(8,128)(2,1)S(1)} %copy.263) | copy-start | bytes 2359300
  448.8 20.9 %copy-start.21 = (bf16[1,512,768]{2,1,0:T(8,128)(2,1)}, bf16[1,512,768]{2,1,0:T(8,128)(2,1)S(1)}, u32[]{:S(2)}) copy-start(bf16[1,512,768]{2,1,0:T(8,128)(2,1)S(1)} %copy.254) | copy-start | bytes 2359300
  463.3 99.6 %reduce-scatter.25.cloned.1.call-start = ((), (), s32[]{:S(2)}) async-start(), calls=%async_computation.18 | async-start | bytes 442368
  464.3 138.9 %all-gather.20.cloned.1.call-start = ((), (), s32[]{:S(2)}) async-start(), calls=%async_computation.10 | async-start | bytes 3932160 | tf_op jit(solution)/shard_map/all_gather | solution.py:144
  465.1 201.9 %all-gather.18.cloned.1.call-start = ((), (), s32[]{:S(2)}) async-start(), calls=%async_computation.9 | async-start | bytes 3932160 | tf_op jit(solution)/shard_map/all_gather | solution.py:144
  465.8 265.0 %all-gather.22.cloned.1.call-start = ((), (), s32[]{:S(2)}) async-start(), calls=%async_computation.11 | async-start | bytes 3932160 | tf_op jit(solution)/shard_map/all_gather | solution.py:184
  469.1 2.9 copy-start.37
  474.9 6.2 copy-start.7
  475.0 319.6 %all-gather.24.cloned.1.call-start = ((), (), s32[]{:S(2)}) async-start(), calls=%async_computation.12 | async-start | bytes 3932160 | tf_op jit(solution)/shard_map/all_gather | solution.py:184
  480.9 425.6 %reduce-scatter.19.cloned.1.call-start = ((), (), s32[]{:S(2)}) async-start(), calls=%async_computation.15 | async-start | bytes 4866048
  485.3 3.4 copy-start.20
  485.4 3.4 copy-start.27
  485.4 3.4 copy-start.28
  508.5 5.5 copy-start.12
  508.5 509.5 %reduce-scatter.15.cloned.1.call-start = ((), (), s32[]{:S(2)}) async-start(), calls=%async_computation.13 | async-start | bytes 4866048 | tf_op jit(solution)/shard_map/reduce_scatter | solution.py:203
  508.5 5.4 copy-start.61
  533.6 596.8 %reduce-scatter.17.cloned.1.call-start = ((), (), s32[]{:S(2)}) async-start(), calls=%async_computation.14 | async-start | bytes 4866048 | tf_op jit(solution)/shard_map/reduce_scatter | solution.py:203
  535.0 4.7 copy-start.32
  (17 other events, 30.8 us)
Sparse Core Ops, SparseCore 0:
  10.9 66.3 all-gather.13
  80.8 62.4 all-gather.11
  146.2 62.4 all-gather.15
  446.8 32.6 reduce-scatter.22
  481.6 20.5 reduce-scatter.20
  505.5 32.1 reduce-scatter.24
  539.3 63.8 all-gather.19
  604.8 62.1 all-gather.17
  668.7 62.1 all-gather.21
  732.3 62.1 all-gather.23
  800.9 105.6 reduce-scatter.18
  911.9 106.0 reduce-scatter.14
  1024.3 106.0 reduce-scatter.16

commit v2 on v1

v2 whole, which is shorter than its diff:
```python
import functools

import jax
import jax.numpy as jnp
from jax import lax
from jax.experimental import pallas as pl
from jax.experimental.pallas import tpu as pltpu
from jax.sharding import PartitionSpec as P

HEAD_DIM = 64
EPSILON = 1e-12
VMEM_LIMIT = 60 * 1024 * 1024
MESH = pl.DeviceIdType.MESH
GATHER_LAG = 1
REDUCE_LAG = 1
LOW = jnp.bfloat16
WIDE = jnp.float32
CHUNK_HEADS = 3
VALUE_AT = (6, 7, 10)
OUT_AT = (8, 9, 11)


def dot_nn(left, right):
    return lax.dot_general(left, right, (((1,), (0,)), ((), ())), preferred_element_type=WIDE)


def dot_nt(left, right):
    return lax.dot_general(left, right, (((1,), (1,)), ((), ())), preferred_element_type=WIDE)


def dot_tn(left, right):
    return lax.dot_general(left, right, (((0,), (0,)), ((), ())), preferred_element_type=WIDE)


def piece(tile, at):
    return tile[:, at * HEAD_DIM : (at + 1) * HEAD_DIM]


def slot_codes(layout, micro, block, slot_count, shape, axis):
    bucket, lengths, counts = layout
    position = lax.broadcasted_iota(jnp.int32, shape, axis)
    quarter = slot_count // 4
    whole = bucket[micro, block] == 1
    item = jnp.where(whole, 0, position // quarter)
    place = position - item * quarter
    length = jnp.where(
        item == 0,
        lengths[micro, block, 0],
        jnp.where(
            item == 1,
            lengths[micro, block, 1],
            jnp.where(item == 2, lengths[micro, block, 2], lengths[micro, block, 3]),
        ),
    )
    return item, (item < counts[micro, block]) & (place < length)


def normalize(hidden):
    center = hidden - jnp.mean(hidden, axis=-1, keepdims=True)
    inverse = lax.rsqrt(jnp.mean(center * center, axis=-1, keepdims=True) + EPSILON)
    return center * inverse, inverse


def norm_pullback(grad_rows, normed, inverse, gain_row):
    grad_normed = grad_rows * gain_row
    return inverse * (
        grad_normed
        - jnp.mean(grad_normed, axis=-1, keepdims=True)
        - normed * jnp.mean(grad_normed * normed, axis=-1, keepdims=True)
    )


def row_sum(values):
    return jnp.sum(values, axis=0, keepdims=True)


def attend_kernel(micro, place, bucket, lengths, counts, x_ref, w_ref, bias_ref, vec_ref,
                  normed_ref, inverse_ref, proj_ref, prob_ref, context_ref, total):
    step = pl.program_id(0)
    slot_count = x_ref.shape[1]
    layout = (bucket, lengths, counts)
    tokens = x_ref[0]
    proj = (dot_nn(tokens, w_ref[0, 0]) + bias_ref[0]).astype(LOW)
    proj_ref[0] = proj
    row_item, _ = slot_codes(layout, micro, place[0], slot_count, (slot_count, 1), 0)
    key_item, key_live = slot_codes(layout, micro, place[0], slot_count, (1, slot_count), 1)
    key_code = jnp.where(key_live, key_item, -1)
    parts = []
    for head in range(CHUNK_HEADS):
        query = piece(proj, 2 * head) * jnp.asarray(HEAD_DIM ** (-0.5), LOW)
        scores = dot_nt(query, piece(proj, 2 * head + 1))
        scores = jnp.where(row_item == key_code, scores, -10000.0)
        grown = jnp.exp(scores - jnp.max(scores, axis=-1, keepdims=True))
        probs = (grown * (1.0 / jnp.sum(grown, axis=-1, keepdims=True))).astype(LOW)
        prob_ref[head] = probs
        parts.append(dot_nn(probs, piece(proj, VALUE_AT[head])).astype(LOW))
    context = jnp.concatenate([parts[0], parts[1], jnp.zeros_like(parts[0]), parts[2]], axis=1)
    context_ref[0] = context
    attention = dot_nt(context, w_ref[0, 0, :, 8 * HEAD_DIM :])

    @pl.when(step == 0)
    def _():
        total[...] = attention

    @pl.when(step > 0)
    def _():
        total[...] += attention

    @pl.when(step == pl.num_programs(0) - 1)
    def _():
        normed, inverse = normalize(tokens.astype(WIDE) + total[...] + vec_ref[2:3])
        normed_ref[...] = normed
        inverse_ref[...] = jnp.broadcast_to(inverse, inverse_ref.shape)


def ffn_kernel(micro, place, bucket, lengths, counts, normed_ref, cot_ref, w_in_ref, w_down_ref, bias_ref, vec_ref,
               act_ref, slope_ref, out_ref, second_ref, second_low_ref, stat_ref, first_low, total):
    step = pl.program_id(0)
    slot_count = normed_ref.shape[0]

    @pl.when(step == 0)
    def _():
        first_low[...] = (normed_ref[...] * vec_ref[0:1] + vec_ref[3:4]).astype(LOW)

    upward = dot_nn(first_low[...], w_in_ref[0, 0]) + bias_ref[0]
    share = 0.5 + 0.5 * lax.erf(upward * (0.5**0.5))
    activated = (upward * share).astype(LOW)
    act_ref[0] = activated
    bell = jnp.exp(-0.5 * upward * upward) * 0.3989422804014327
    slope_ref[0] = (share + upward * bell).astype(LOW)
    down = dot_nt(activated, w_down_ref[0, 0])

    @pl.when(step == 0)
    def _():
        total[...] = down

    @pl.when(step > 0)
    def _():
        total[...] += down

    @pl.when(step == pl.num_programs(0) - 1)
    def _():
        _, live = slot_codes((bucket, lengths, counts), micro, place[0], slot_count, (slot_count, 1), 0)
        first = normed_ref[...] * vec_ref[0:1] + vec_ref[3:4]
        normed, inverse = normalize(first + total[...] + vec_ref[4:5])
        out_ref[...] = (normed * vec_ref[1:2] + vec_ref[5:6]).astype(LOW)
        grad_out = jnp.where(live, cot_ref[0].astype(WIDE), 0.0)
        second = norm_pullback(grad_out, normed, inverse, vec_ref[1:2])
        second_ref[...] = second
        second_low_ref[...] = second.astype(LOW)
        stat_ref[...] = jnp.concatenate(
            [row_sum(grad_out * normed), row_sum(grad_out), row_sum(second), jnp.zeros((5, second.shape[1]), WIDE)], axis=0
        )


def ffn_back_kernel(second_ref, second_low_ref, slope_ref, w_in_ref, w_down_ref, normed_ref, inverse_ref, vec_ref,
                    up_ref, hidden_ref, hidden_low_ref, up_stat_ref, stat_ref, total):
    step = pl.program_id(0)
    grad_act = dot_nn(second_low_ref[...], w_down_ref[0, 0])
    grad_up = (grad_act * slope_ref[0].astype(WIDE)).astype(LOW)
    up_ref[0] = grad_up
    up_stat_ref[0] = jnp.broadcast_to(row_sum(grad_up.astype(WIDE)), up_stat_ref.shape[1:])
    back = dot_nt(grad_up, w_in_ref[0, 0])

    @pl.when(step == 0)
    def _():
        total[...] = back + second_ref[...]

    @pl.when(step > 0)
    def _():
        total[...] += back

    @pl.when(step == pl.num_programs(0) - 1)
    def _():
        grad_first = total[...]
        normed = normed_ref[...]
        hidden = norm_pullback(grad_first, normed, inverse_ref[:, :1], vec_ref[0:1])
        hidden_ref[...] = hidden
        hidden_low_ref[...] = hidden.astype(LOW)
        stat_ref[...] = jnp.concatenate(
            [row_sum(grad_first * normed), row_sum(grad_first), row_sum(hidden), jnp.zeros((5, hidden.shape[1]), WIDE)],
            axis=0,
        )


def attend_back_kernel(micro, place, bucket, lengths, counts, hidden_ref, hidden_low_ref, w_ref, proj_ref, prob_ref,
                       context_ref, grad_ref, out_ref, stat_ref, total):
    step = pl.program_id(0)
    slot_count = hidden_ref.shape[0]
    layout = (bucket, lengths, counts)
    row_item, _ = slot_codes(layout, micro, place[0], slot_count, (slot_count, 1), 0)
    key_item, key_live = slot_codes(layout, micro, place[0], slot_count, (1, slot_count), 1)
    key_code = jnp.where(key_live, key_item, -1)
    proj = proj_ref[0]
    grad_context = dot_nn(hidden_low_ref[...], w_ref[0, 0, :, 8 * HEAD_DIM :]).astype(LOW)
    scale = HEAD_DIM ** (-0.5)
    grads = [None] * 12
    for head in range(CHUNK_HEADS):
        query, key = piece(proj, 2 * head), piece(proj, 2 * head + 1)
        probs = prob_ref[head]
        grad_head = piece(grad_context, OUT_AT[head] - 8)
        grads[VALUE_AT[head]] = dot_tn(probs, grad_head).astype(LOW)
        grad_probs = dot_nt(grad_head, piece(proj, VALUE_AT[head]))
        wide = probs.astype(WIDE)
        inner = jnp.sum(wide * grad_probs, axis=-1, keepdims=True)
        grad_scores = jnp.where(row_item == key_code, wide * (grad_probs - inner), 0.0).astype(LOW)
        grads[2 * head] = (dot_nn(grad_scores, key) * scale).astype(LOW)
        grads[2 * head + 1] = (dot_tn(grad_scores, query) * scale).astype(LOW)
    context = context_ref[0]
    zero = jnp.zeros_like(grads[0])
    for at in OUT_AT:
        grads[at] = zero
    slab = jnp.concatenate(grads, axis=1)
    back = dot_nt(slab, w_ref[0, 0])
    for at in OUT_AT:
        grads[at] = piece(context, at - 8)
    grad_ref[0] = jnp.concatenate(grads, axis=1)
    stat_ref[0] = jnp.broadcast_to(row_sum(slab.astype(WIDE)), stat_ref.shape[1:])

    @pl.when(step == 0)
    def _():
        total[...] = back + hidden_ref[...]

    @pl.when(step > 0)
    def _():
        total[...] += back

    @pl.when(step == pl.num_programs(0) - 1)
    def _():
        out_ref[...] = total[...].astype(LOW)


def in_vmem(shape, index_map):
    return pl.BlockSpec(shape, index_map)


def params(vmem=VMEM_LIMIT):
    return pltpu.CompilerParams(dimension_semantics=("arbitrary",), vmem_limit_bytes=vmem)


def attend(micro, place, bucket, lengths, counts, inputs, weights, bias, vectors, slot_count):
    parts, width = weights.shape[1], weights.shape[2]
    wide_slab = weights.shape[3]
    heads = parts * CHUNK_HEADS
    whole = lambda *shape: pl.BlockSpec(shape, lambda j, p, b, l, c: (0,) * len(shape))
    return pl.pallas_call(
        functools.partial(attend_kernel, micro),
        grid_spec=pltpu.PrefetchScalarGridSpec(
            num_scalar_prefetch=4,
            grid=(parts,),
            in_specs=[
                pl.BlockSpec((1, slot_count, width), lambda j, p, b, l, c: (micro, p[0], 0)),
                pl.BlockSpec((1, 1, width, wide_slab), lambda j, p, b, l, c: (0, j, 0, 0)),
                pl.BlockSpec((1, 1, wide_slab), lambda j, p, b, l, c: (j, 0, 0)),
                whole(*vectors.shape),
            ],
            out_specs=[
                whole(slot_count, width),
                whole(slot_count, 128),
                pl.BlockSpec((1, slot_count, wide_slab), lambda j, p, b, l, c: (j, 0, 0)),
                pl.BlockSpec((CHUNK_HEADS, slot_count, slot_count), lambda j, p, b, l, c: (j, 0, 0)),
                pl.BlockSpec((1, slot_count, 4 * HEAD_DIM), lambda j, p, b, l, c: (j, 0, 0)),
            ],
            scratch_shapes=[pltpu.VMEM((slot_count, width), WIDE)],
        ),
        out_shape=[
            jax.ShapeDtypeStruct((slot_count, width), WIDE),
            jax.ShapeDtypeStruct((slot_count, 128), WIDE),
            jax.ShapeDtypeStruct((parts, slot_count, wide_slab), LOW),
            jax.ShapeDtypeStruct((heads, slot_count, slot_count), LOW),
            jax.ShapeDtypeStruct((parts, slot_count, 4 * HEAD_DIM), LOW),
        ],
        compiler_params=params(),
        name="attend",
    )(place, bucket, lengths, counts, inputs, weights, bias, vectors)


def ffn(micro, place, bucket, lengths, counts, normed, cotangent, weights, bias, vectors):
    parts, width, cols = weights.shape[1:]
    slot_count = normed.shape[0]
    whole = lambda *shape: pl.BlockSpec(shape, lambda j, p, b, l, c: (0,) * len(shape))
    each = pl.BlockSpec((1, slot_count, cols), lambda j, p, b, l, c: (j, 0, 0))
    return pl.pallas_call(
        functools.partial(ffn_kernel, micro),
        grid_spec=pltpu.PrefetchScalarGridSpec(
            num_scalar_prefetch=4,
            grid=(parts,),
            in_specs=[
                whole(slot_count, width),
                pl.BlockSpec((1, slot_count, width), lambda j, p, b, l, c: (micro, p[0], 0)),
                pl.BlockSpec((1, 1, width, cols), lambda j, p, b, l, c: (1, j, 0, 0)),
                pl.BlockSpec((1, 1, width, cols), lambda j, p, b, l, c: (2, j, 0, 0)),
                pl.BlockSpec((1, 1, cols), lambda j, p, b, l, c: (j, 0, 0)),
                whole(*vectors.shape),
            ],
            out_specs=[each, each, whole(slot_count, width), whole(slot_count, width), whole(slot_count, width), whole(8, width)],
            scratch_shapes=[pltpu.VMEM((slot_count, width), LOW), pltpu.VMEM((slot_count, width), WIDE)],
        ),
        out_shape=[
            jax.ShapeDtypeStruct((parts, slot_count, cols), LOW),
            jax.ShapeDtypeStruct((parts, slot_count, cols), LOW),
            jax.ShapeDtypeStruct((slot_count, width), LOW),
            jax.ShapeDtypeStruct((slot_count, width), WIDE),
            jax.ShapeDtypeStruct((slot_count, width), LOW),
            jax.ShapeDtypeStruct((8, width), WIDE),
        ],
        compiler_params=params(),
        name="ffn",
    )(place, bucket, lengths, counts, normed, cotangent, weights, weights, bias, vectors)


def ffn_back(second, second_low, slope, weights, normed, inverse, vectors):
    parts, width, cols = weights.shape[1:]
    slot_count = normed.shape[0]
    whole = lambda *shape: pl.BlockSpec(shape, lambda j: (0,) * len(shape))
    each = pl.BlockSpec((1, slot_count, cols), lambda j: (j, 0, 0))
    return pl.pallas_call(
        ffn_back_kernel,
        grid=(parts,),
        in_specs=[
            whole(slot_count, width),
            whole(slot_count, width),
            each,
            pl.BlockSpec((1, 1, width, cols), lambda j: (1, j, 0, 0)),
            pl.BlockSpec((1, 1, width, cols), lambda j: (2, j, 0, 0)),
            whole(slot_count, width),
            whole(slot_count, 128),
            whole(*vectors.shape),
        ],
        out_specs=[each, whole(slot_count, width), whole(slot_count, width),
                   pl.BlockSpec((1, 8, cols), lambda j: (j, 0, 0)), whole(8, width)],
        scratch_shapes=[pltpu.VMEM((slot_count, width), WIDE)],
        out_shape=[
            jax.ShapeDtypeStruct((parts, slot_count, cols), LOW),
            jax.ShapeDtypeStruct((slot_count, width), WIDE),
            jax.ShapeDtypeStruct((slot_count, width), LOW),
            jax.ShapeDtypeStruct((parts, 8, cols), WIDE),
            jax.ShapeDtypeStruct((8, width), WIDE),
        ],
        compiler_params=params(),
        name="ffn_back",
    )(second, second_low, slope, weights, weights, normed, inverse, vectors)


def attend_back(micro, place, bucket, lengths, counts, hidden, hidden_low, weights, proj, probs, context):
    parts, width = weights.shape[1], weights.shape[2]
    wide_slab = weights.shape[3]
    slot_count = hidden.shape[0]
    whole = lambda *shape: pl.BlockSpec(shape, lambda j, p, b, l, c: (0,) * len(shape))
    each = pl.BlockSpec((1, slot_count, wide_slab), lambda j, p, b, l, c: (j, 0, 0))
    return pl.pallas_call(
        functools.partial(attend_back_kernel, micro),
        grid_spec=pltpu.PrefetchScalarGridSpec(
            num_scalar_prefetch=4,
            grid=(parts,),
            in_specs=[
                whole(slot_count, width),
                whole(slot_count, width),
                pl.BlockSpec((1, 1, width, wide_slab), lambda j, p, b, l, c: (0, j, 0, 0)),
                each,
                pl.BlockSpec((CHUNK_HEADS, slot_count, slot_count), lambda j, p, b, l, c: (j, 0, 0)),
                pl.BlockSpec((1, slot_count, 4 * HEAD_DIM), lambda j, p, b, l, c: (j, 0, 0)),
            ],
            out_specs=[each, whole(slot_count, width), pl.BlockSpec((1, 8, wide_slab), lambda j, p, b, l, c: (j, 0, 0))],
            scratch_shapes=[pltpu.VMEM((slot_count, width), WIDE)],
        ),
        out_shape=[
            jax.ShapeDtypeStruct((parts, slot_count, wide_slab), LOW),
            jax.ShapeDtypeStruct((slot_count, width), LOW),
            jax.ShapeDtypeStruct((parts, 8, wide_slab), WIDE),
        ],
        compiler_params=params(),
        name="attend_back",
    )(place, bucket, lengths, counts, hidden, hidden_low, weights, proj, probs, context)


def weight_grads_kernel(blocks, place, *refs):
    normed = refs[:blocks]
    second_low, hidden_low, act, grad_up, head_grads, tokens = [refs[(k + 1) * blocks : (k + 2) * blocks] for k in range(6)]
    vec_ref, out_ref = refs[7 * blocks], refs[7 * blocks + 1]
    turned = refs[7 * blocks + 2]
    step = pl.program_id(0)
    slot_count = second_low[0].shape[0]

    @pl.when(step == 0)
    def _():
        for b in range(blocks):
            span = slice(b * slot_count, (b + 1) * slot_count)
            first = (normed[b][...] * vec_ref[0:1] + vec_ref[3:4]).astype(LOW)
            turned[0, :, span] = tokens[b][0].T
            turned[1, :, span] = first.T
            turned[2, :, span] = second_low[b][...].T
            turned[3, :, span] = hidden_low[b][...].T

    grads = jnp.concatenate([ref[0] for ref in head_grads], axis=0)
    qkv = dot_nn(turned[0], grads)
    outs = dot_nn(turned[3], grads[:, 8 * HEAD_DIM :])
    lane = lax.broadcasted_iota(jnp.int32, (1, 2 * HEAD_DIM), 1)
    last = jnp.where(lane < HEAD_DIM, qkv[:, 10 * HEAD_DIM :], outs[:, 2 * HEAD_DIM :])
    out_ref[0, 0] = jnp.concatenate([qkv[:, : 8 * HEAD_DIM], outs[:, : 2 * HEAD_DIM], last], axis=1).astype(LOW)
    out_ref[1, 0] = dot_nn(turned[1], jnp.concatenate([ref[0] for ref in grad_up], axis=0)).astype(LOW)
    out_ref[2, 0] = dot_nn(turned[2], jnp.concatenate([ref[0] for ref in act], axis=0)).astype(LOW)


def weight_grads(place, inputs, normed, second_low, hidden_low, act, grad_up, head_grads, vectors):
    blocks = len(normed)
    micro_count = inputs.shape[0]
    per_micro = blocks // micro_count
    parts, slot_count, cols = act[0].shape
    width = normed[0].shape[1]
    whole = lambda *shape: pl.BlockSpec(shape, lambda j, p: (0,) * len(shape))
    each = pl.BlockSpec((1, slot_count, cols), lambda j, p: (j, 0, 0))
    token_specs = [
        pl.BlockSpec((1, slot_count, width), lambda j, p, m=b // per_micro, k=b % per_micro: (m, p[0] + k, 0))
        for b in range(blocks)
    ]
    return pl.pallas_call(
        functools.partial(weight_grads_kernel, blocks),
        grid_spec=pltpu.PrefetchScalarGridSpec(
            num_scalar_prefetch=1,
            grid=(parts,),
            in_specs=[whole(slot_count, width)] * (3 * blocks) + [each] * (3 * blocks) + token_specs + [whole(*vectors.shape)],
            out_specs=pl.BlockSpec((3, 1, width, cols), lambda j, p: (0, j, 0, 0)),
            scratch_shapes=[pltpu.VMEM((4, width, blocks * slot_count), LOW)],
        ),
        out_shape=jax.ShapeDtypeStruct((3, parts, width, cols), LOW),
        compiler_params=params(),
        name="weight_grads",
    )(place, *normed, *second_low, *hidden_low, *act, *grad_up, *head_grads, *([inputs] * blocks), vectors)


def mesh_place(bits):
    d = lax.axis_index("dp")
    t = lax.axis_index("tensor")
    digits = [(d // (1 << k)) % 2 for k in range(bits)]
    mates = [d + (1 - 2 * digits[k]) * (1 << k) for k in range(bits)]
    return d, t, digits, mates


def digit_index(bits, digits, open_bits):
    return tuple(slice(None) if k in open_bits else digits[k] for k in reversed(range(bits)))


def greet(d, t, mates, parts):
    barrier = pltpu.get_barrier_semaphore()
    for mate in mates:
        pl.semaphore_signal(barrier, inc=1, device_id=(mate, t), device_id_type=MESH)
    for hop in range(1, parts):
        pl.semaphore_signal(barrier, inc=1, device_id=(d, (t + hop) % parts), device_id_type=MESH)
    pl.semaphore_wait(barrier, len(mates) + parts - 1)


def bit_order(bits, flip):
    far = list(range(1, bits))
    return (far[::-1] if flip else far) + [0]


def gather_kernel(parts, bits, own, small, full, small_dp, small_t, z_send, z_recv, h_send, h_recv, s_send, s_recv, keep):
    d, t, digits, mates = mesh_place(bits)
    slab_count = own.shape[0]
    mine = digit_index(bits, digits, ())
    greet(d, t, mates, parts)
    offsets = [0] + [sign * hop for hop in range(1, parts) for sign in (1, -1)]
    pending = []

    def remote(src, dst, send, recv, to):
        return pltpu.make_async_remote_copy(src, dst, send, recv, device_id=to, device_id_type=MESH)

    local = [pltpu.make_async_copy(own.at[s], full.at[(s, t) + mine], keep.at[s]) for s in range(slab_count)]
    local.append(pltpu.make_async_copy(small.at[0], small_dp.at[mine], keep.at[slab_count]))
    local.append(pltpu.make_async_copy(small.at[1], small_t.at[t], keep.at[slab_count + 1]))
    for copy in local:
        copy.start()

    def z_copy(s, at, src, up):
        to = (d, t + 1) if up else (d, t - 1)
        way = 0 if up else 1
        return remote(src, full.at[(s, at) + mine], z_send.at[s, at, way], z_recv.at[s, at], to)

    def h_copy(s, index, step):
        offset = offsets[index]
        order = bit_order(bits, (abs(offset) + s) % 2 == 1)
        blocks = (s, t + offset) + digit_index(bits, digits, order[:step])
        src = own.at[s] if offset == 0 and step == 0 else full.at[blocks]
        return remote(src, full.at[blocks], h_send.at[s, index, step], h_recv.at[s, index, step], (mates[order[step]], t))

    def exists(offset):
        return (t + offset >= 0) & (t + offset < parts)

    def begin(s, index):
        offset = offsets[index]
        if offset == 0:
            h_copy(s, index, 0).start()
            return

        @pl.when(exists(offset))
        def _():
            up = offset < 0
            z_copy(s, t + offset, own.at[s], up).wait_recv()

            @pl.when((t < parts - 1) if up else (t > 0))
            def _():
                z_copy(s, t + offset, full.at[(s, t + offset) + mine], up).start()

            h_copy(s, index, 0).start()

    def advance(s, index, step):
        @pl.when(exists(offsets[index]))
        def _():
            h_copy(s, index, step - 1).wait_recv()
            if step < bits:
                h_copy(s, index, step).start()

    def small_step(step):
        blocks = digit_index(bits, digits, range(step))
        src = small.at[0] if step == 0 else small_dp.at[blocks]
        return remote(src, small_dp.at[blocks], s_send.at[step], s_recv.at[step], (mates[step], t))

    def small_hop(hop):
        peer = (d, (t + hop) % parts)
        return remote(small.at[1], small_t.at[t], s_send.at[bits + hop - 1], s_recv.at[bits + hop - 1], peer)

    for s in range(slab_count):
        @pl.when(t < parts - 1)
        def _():
            z_copy(s, t, own.at[s], True).start()

        @pl.when(t > 0)
        def _():
            z_copy(s, t, own.at[s], False).start()
        if s == 0:
            begin(0, 0)
            for hop in range(1, parts):
                small_hop(hop).start()
            small_step(0).start()
    for copy in local:
        copy.wait()

    groups = [(s, [index for index, offset in enumerate(offsets) if abs(offset) == hop])
              for s in range(slab_count) for hop in range(parts)]
    for wave in range(len(groups) + bits * GATHER_LAG):
        for step in range(bits + 1):
            if 0 <= wave - step * GATHER_LAG < len(groups):
                s, indices = groups[wave - step * GATHER_LAG]
                for index in indices:
                    if step:
                        advance(s, index, step)
                    elif (s, index) != (0, 0):
                        begin(s, index)
        if wave < bits:
            small_step(wave).wait_recv()
            if wave + 1 < bits:
                small_step(wave + 1).start()

    for hop in range(1, parts):
        small_hop(hop).wait()
    for step in range(bits):
        small_step(step).wait_send()
    for s, indices in groups:
        for index in indices:
            offset = offsets[index]

            @pl.when(exists(offset))
            def _():
                for step in range(bits):
                    h_copy(s, index, step).wait_send()
                if offset <= 0:
                    @pl.when(t < parts - 1)
                    def _():
                        z_copy(s, t + offset, own.at[s], True).wait_send()
                if offset >= 0:
                    @pl.when(t > 0)
                    def _():
                        z_copy(s, t + offset, own.at[s], False).wait_send()


def gather_weights(own, small, parts, dp_count):
    bits = dp_count.bit_length() - 1
    slab_count, rows, columns = own.shape
    places = 2 * parts - 1
    low = jnp.bfloat16
    full, small_dp, small_t = pl.pallas_call(
        functools.partial(gather_kernel, parts, bits),
        out_shape=[
            jax.ShapeDtypeStruct((slab_count, parts) + (2,) * bits + (rows, columns), low),
            jax.ShapeDtypeStruct((2,) * bits + small.shape[1:], low),
            jax.ShapeDtypeStruct((parts,) + small.shape[1:], low),
        ],
        in_specs=[pl.BlockSpec(memory_space=pl.ANY)] * 2,
        out_specs=[pl.BlockSpec(memory_space=pl.ANY)] * 3,
        scratch_shapes=[
            pltpu.SemaphoreType.DMA((slab_count, parts, 2)),
            pltpu.SemaphoreType.DMA((slab_count, parts)),
            pltpu.SemaphoreType.DMA((slab_count, places, bits)),
            pltpu.SemaphoreType.DMA((slab_count, places, bits)),
            pltpu.SemaphoreType.DMA((bits + parts - 1,)),
            pltpu.SemaphoreType.DMA((bits + parts - 1,)),
            pltpu.SemaphoreType.DMA((slab_count + 2,)),
        ],
        compiler_params=pltpu.CompilerParams(collective_id=0, has_side_effects=True, vmem_limit_bytes=VMEM_LIMIT),
        name="gather_weights",
    )(own, small)
    full = full.reshape(slab_count, parts, dp_count * rows, columns)
    return full, small_dp.reshape((dp_count,) + small.shape[1:]), small_t


def add_rows(target, first, second, rows):
    lead = target.shape[:-2]
    chunk = 16 if rows % 16 == 0 else rows
    steps = rows // chunk
    count = 1
    for extent in lead:
        count *= extent

    def one(i, carry):
        at, rest = [], i // steps
        for extent in reversed(lead):
            at.insert(0, rest % extent)
            rest = rest // extent
        where = tuple(at) + (pl.ds(pl.multiple_of((i % steps) * chunk, chunk), chunk),)
        total = first[where].astype(jnp.float32) + second[where].astype(jnp.float32)
        target[where] = total.astype(target.dtype)
        return carry

    lax.fori_loop(0, count * steps, one, 0)


def reduce_kernel(parts, bits, grads, small, out, small_out, *scratch):
    bufs = scratch[:bits]
    z_up, z_down, small_buf, small_sum = scratch[bits:bits + 4]
    h_send, h_recv, up_send, up_recv, down_send, down_recv, s_send, s_recv = scratch[bits + 4:]
    d, t, digits, mates = mesh_place(bits)
    slab_count = grads.shape[0]
    rows = grads.shape[-2]
    greet(d, t, mates, parts)
    items = [(s, at) for s in range(slab_count) for at in range(parts)]
    small_bits = bits + parts.bit_length() - 1

    def remote(src, dst, send, recv, to):
        return pltpu.make_async_remote_copy(src, dst, send, recv, device_id=to, device_id_type=MESH)

    def order_of(number):
        s, at = items[number]
        return bit_order(bits, (s + at) % 2 == 1)[::-1]

    def held(number, step):
        s, at = items[number]
        return grads.at[s, at] if step == 0 else bufs[step - 1].at[number]

    def part_of(number, step, side):
        order = order_of(number)
        left = [k for k in reversed(range(bits)) if k not in order[:step]]
        pick = tuple(side if k == order[step] else slice(None) for k in left)
        return held(number, step).at[pick]

    def h_copy(number, step):
        order = order_of(number)
        digit = digits[order[step]]
        return remote(part_of(number, step, 1 - digit), bufs[step].at[number],
                      h_send.at[number, step], h_recv.at[number, step], (mates[order[step]], t))

    def fold(number, step):
        h_copy(number, step).wait_recv()
        digit = digits[order_of(number)[step]]
        add_rows(bufs[step].at[number], bufs[step].at[number], part_of(number, step, digit), rows)

    def summed(s, at):
        return bufs[bits - 1].at[s * parts + at]

    def z_copy(s, at, up, src):
        buf, send, recv = (z_up, up_send, up_recv) if up else (z_down, down_send, down_recv)
        to = (d, t + 1) if up else (d, t - 1)
        return remote(src, buf.at[s, at], send.at[s, at], recv.at[s, at], to)

    def z_pass(s, hop, up):
        at = t + hop if up else t - hop
        edge = (t == 0) if up else (t == parts - 1)
        buf = z_up if up else z_down

        @pl.when((at < parts) if up else (at >= 0))
        def _():
            @pl.when(edge)
            def _():
                z_copy(s, at, up, summed(s, at)).start()

            @pl.when(jnp.logical_not(edge))
            def _():
                z_copy(s, at, up, summed(s, at)).wait_recv()
                add_rows(buf.at[s, at], buf.at[s, at], summed(s, at), rows)
                z_copy(s, at, up, buf.at[s, at]).start()

    def z_finish(s):
        add_rows(out.at[s], summed(s, t), summed(s, t), rows)

        def scaled(i, carry):
            out[s] = out[s] * 0.5
            return carry
        lax.fori_loop(0, 1, scaled, 0)
        for up, buf in ((True, z_up), (False, z_down)):
            @pl.when((t > 0) if up else (t < parts - 1))
            def _():
                z_copy(s, t, up, summed(s, t)).wait_recv()
                add_rows(out.at[s], out.at[s], buf.at[s, t], rows)

    def small_copy(step):
        if step < bits:
            to = (mates[step], t)
        else:
            gap = 1 << (step - bits)
            to = (d, t + (1 - 2 * ((t // gap) % 2)) * gap)
        src = small if step == 0 else small_sum.at[step - 1]
        return remote(src, small_buf.at[step], s_send.at[step], s_recv.at[step], to)

    def small_fold(step):
        small_copy(step).wait_recv()
        before = small[...] if step == 0 else small_sum[step - 1]
        small_sum[step] = before + small_buf[step]
        if step + 1 < small_bits:
            small_copy(step + 1).start()

    for number in range(len(items)):
        h_copy(number, 0).start()
        if number == 0:
            small_copy(0).start()
    for wave in range(len(items) + bits * REDUCE_LAG + parts + 1):
        for step in range(bits):
            number = wave - step * REDUCE_LAG
            if 0 <= number < len(items):
                fold(number, step)
                if step + 1 < bits:
                    h_copy(number, step + 1).start()
        for s in range(slab_count):
            phase = wave - ((s + 1) * parts - 1 + bits * REDUCE_LAG)
            if 0 <= phase < parts - 1:
                z_pass(s, parts - 1 - phase, True)
                z_pass(s, parts - 1 - phase, False)
            elif phase == parts - 1:
                z_finish(s)
        if wave < small_bits:
            small_fold(wave)
    small_out[...] = small_sum[small_bits - 1]

    for step in range(small_bits):
        small_copy(step).wait_send()
    for number in range(len(items)):
        for step in range(bits):
            h_copy(number, step).wait_send()
    for s in range(slab_count):
        for hop in range(1, parts):
            @pl.when(t + hop < parts)
            def _():
                z_copy(s, t + hop, True, summed(s, t)).wait_send()

            @pl.when(t - hop >= 0)
            def _():
                z_copy(s, t - hop, False, summed(s, t)).wait_send()


def reduce_grads(grads, small, parts, dp_count):
    bits = dp_count.bit_length() - 1
    slab_count, columns = grads.shape[0], grads.shape[-1]
    rows = grads.shape[2] // dp_count
    grads = grads.reshape((slab_count, parts) + (2,) * bits + (rows, columns))
    low = jnp.bfloat16
    count = slab_count * parts
    small_bits = bits + parts.bit_length() - 1
    dma = pltpu.SemaphoreType.DMA
    return pl.pallas_call(
        functools.partial(reduce_kernel, parts, bits),
        out_shape=[
            jax.ShapeDtypeStruct((slab_count, rows, columns), jnp.float32),
            jax.ShapeDtypeStruct(small.shape, jnp.float32),
        ],
        in_specs=[pl.BlockSpec(memory_space=pltpu.VMEM)] * 2,
        out_specs=[pl.BlockSpec(memory_space=pltpu.VMEM)] * 2,
        scratch_shapes=[pltpu.VMEM((count,) + (2,) * (bits - 1 - step) + (rows, columns), low) for step in range(bits)]
        + [pltpu.VMEM((slab_count, parts, rows, columns), low)] * 2
        + [pltpu.VMEM((small_bits,) + small.shape, jnp.float32)] * 2
        + [dma((count, bits)), dma((count, bits))]
        + [dma((slab_count, parts))] * 4
        + [dma((small_bits,))] * 2,
        compiler_params=pltpu.CompilerParams(collective_id=1, has_side_effects=True, vmem_limit_bytes=VMEM_LIMIT),
        name="reduce_grads",
    )(grads, small)


def slab_order(query, key, value, out):
    columns = lambda group, head: group[..., head * HEAD_DIM : (head + 1) * HEAD_DIM]
    order = [(query, 0), (key, 0), (query, 1), (key, 1), (query, 2), (key, 2),
             (value, 0), (value, 1), (out, 0), (out, 1), (value, 2), (out, 2)]
    return jnp.concatenate([columns(group, head) for group, head in order], axis=-1)


def slab_parts(slab):
    columns = lambda at: slab[..., at * HEAD_DIM : (at + 1) * HEAD_DIM]
    groups = ((0, 2, 4), (1, 3, 5), VALUE_AT, OUT_AT)
    return [jnp.concatenate([columns(at) for at in group], axis=-1) for group in groups]


def add_all(terms):
    total = terms[0]
    for term in terms[1:]:
        total = total + term
    return total


def body(
    inputs,
    cotangent,
    bucket,
    lengths,
    counts,
    w_qkv,
    w_out,
    w_in,
    w_down,
    head_bias,
    ffn_bias,
    norm_gains,
    row_biases,
):
    micro_count, _, width = inputs.shape
    blocks_all = bucket.shape[1]
    slot_count = inputs.shape[1] // blocks_all
    parts, dp_count = lax.axis_size("tensor"), lax.axis_size("dp")
    rank, dp_rank = lax.axis_index("tensor"), lax.axis_index("dp")
    per_micro = blocks_all // parts
    cols = w_in.shape[1]
    rows = w_in.shape[0]

    own = jnp.stack([slab_order(w_qkv[0], w_qkv[1], w_qkv[2], w_out.T), w_in, w_down.T])
    norm_row = jnp.concatenate([norm_gains, row_biases], axis=0).reshape(1, -1)
    vector_count = norm_gains.shape[0] + row_biases.shape[0]
    no_bias = jnp.zeros_like(head_bias[:1])
    bias_rows = jnp.concatenate([slab_order(head_bias[:1], no_bias, head_bias[1:], no_bias), ffn_bias[None]], axis=0)
    small = jnp.stack([
        jnp.pad(norm_row, ((0, 15), (0, cols - norm_row.shape[1]))),
        jnp.pad(bias_rows, ((0, 14), (0, 0))),
    ])
    weights, small_dp, small_t = gather_weights(own, small, parts, dp_count)
    vectors = small_dp[:, 0, : norm_row.shape[1]].reshape(dp_count, vector_count, rows)
    vectors = vectors.transpose(1, 0, 2).reshape(vector_count, width).astype(jnp.float32)
    vectors = jnp.pad(vectors, ((0, 8 - vector_count), (0, 0)))
    head_rows = small_t[:, 0:1].astype(jnp.float32)
    ffn_rows = small_t[:, 1:2].astype(jnp.float32)

    blocks = [(m, k) for m in range(micro_count) for k in range(per_micro)]
    places = [jnp.full((1,), rank * per_micro + k, jnp.int32) for k in range(per_micro)]
    layout = (bucket, lengths, counts)
    kept = []
    outs = []
    for m, k in blocks:
        normed, inverse, proj, probs, context = attend(m, places[k], *layout, inputs, weights, head_rows, vectors, slot_count)
        act, slope, out, second, second_low, stat = ffn(m, places[k], *layout, normed, cotangent, weights, ffn_rows, vectors)
        kept.append((normed, inverse, proj, probs, context, act, slope, second, second_low, stat))
        outs.append(out)
    results = [
        lax.all_gather(jnp.concatenate(outs[m * per_micro : (m + 1) * per_micro], axis=0), "tensor", axis=0, tiled=True)
        for m in range(micro_count)
    ]
    token_grads, saved = [], []
    for (m, k), (normed, inverse, proj, probs, context, act, slope, second, second_low, stat) in zip(blocks, kept):
        grad_up, hidden, hidden_low, up_stat, first_stat = ffn_back(second, second_low, slope, weights, normed, inverse, vectors)
        head_grads, token_grad, head_stat = attend_back(
            m, places[k], *layout, hidden, hidden_low, weights, proj, probs, context
        )
        token_grads.append(token_grad)
        saved.append((normed, second_low, hidden_low, act, grad_up, head_grads, stat, first_stat, up_stat, head_stat))
    input_grads = [
        lax.all_gather(jnp.concatenate(token_grads[m * per_micro : (m + 1) * per_micro], axis=0), "tensor", axis=0, tiled=True)
        for m in range(micro_count)
    ]
    columns = list(zip(*saved))
    grads = weight_grads(places[0], inputs, *columns[:6], vectors)
    stat, first_stat, up_stat, head_stat = [add_all(column) for column in columns[6:]]
    small_grads = jnp.concatenate(
        [
            jnp.stack([first_stat[0], stat[0], first_stat[2], first_stat[1], stat[2], stat[1]]),
            up_stat[:, 0],
            head_stat[:, 0],
        ],
        axis=0,
    )
    small_grads = jnp.pad(small_grads, ((0, -small_grads.shape[0] % 8), (0, 0)))
    shard, sums = reduce_grads(grads, small_grads, parts, dp_count)
    grad_query, grad_key, grad_value, grad_out = slab_parts(shard[0])
    vector_sums = lax.dynamic_slice_in_dim(sums[:vector_count], dp_rank * rows, rows, 1)
    ffn_sum = lax.dynamic_slice_in_dim(sums, vector_count + rank, 1, 0)[0]
    head_sum = slab_parts(lax.dynamic_slice_in_dim(sums, vector_count + parts + rank, 1, 0))
    return (
        jnp.stack(results),
        jnp.stack(input_grads),
        jnp.stack([grad_query, grad_key, grad_value]),
        grad_out.T,
        shard[1],
        shard[2].T,
        jnp.concatenate([head_sum[0], head_sum[2]], axis=0),
        ffn_sum,
        vector_sums[:2],
        vector_sums[2:],
    )


def solution(mesh):
    in_specs = (
        P(None, "dp", None),
        P(None, "dp", None),
        P(None, "dp"),
        P(None, "dp", None),
        P(None, "dp"),
        P(None, "dp", "tensor"),
        P("tensor", "dp"),
        P("dp", "tensor"),
        P("tensor", "dp"),
        P(None, "tensor"),
        P("tensor"),
        P(None, "dp"),
        P(None, "dp"),
    )
    out_specs = (
        P(None, "dp", None),
        P(None, "dp", None),
        P(None, "dp", "tensor"),
        P("tensor", "dp"),
        P("dp", "tensor"),
        P("tensor", "dp"),
        P(None, "tensor"),
        P("tensor"),
        P(None, "dp"),
        P(None, "dp"),
    )
    return jax.shard_map(body, mesh=mesh, in_specs=in_specs, out_specs=out_specs, check_vma=False)
```

time: 1140 us -> 498 us (0.44)
  waiting for transfers between devices: 616 us -> 50.3 us
  Pallas kernels: 0 us -> 393 us
  matrix products: 241 us -> 0 us
  local copies, waits for them, and re-layouts: 137 us -> 13.9 us
  blocking collectives: 76.6 us -> 0 us
  other arithmetic: 50.3 us -> 21.2 us
    pallas_call x0 -> x11, Pallas kernels: none -> 393 us  [the longest x1 123 us: reduce_grads(): pl.pallas_call(functools.partial(reduce_kernel, parts, bits), out_shape=[...]
    all_gather x7 -> x4, waiting for transfers between devices: 287 us -> 49.1 us  [the longest x2 49.1 us: body(): lax.all_gather(jnp.concatenate(outs[m * per_micro:(m + 1) * per_micro], a...]
    dot_general x38 -> x0, matrix products: 225 us -> none  [the longest x2 44.1 us: body(): jnp.dot(first_low, mat_in, preferred_element_type=jnp.float32) + hidden_bias]
    reduce_scatter x2 -> x0, waiting for transfers between devices: 220 us -> none  [body(): lax.psum_scatter(v.astype(jnp.bfloat16), both, scatter_dimension=0, tiled...]
    unnamed x17 -> x4, waiting for transfers between devices: 109 us -> 1.24 us
    all_gather x4 -> x0, blocking collectives: 43.5 us -> none  [the longest x1 13 us: body(): lax.all_gather(ffn_bias, 'tensor', axis=0, tiled=True).astype(jnp.float32)]
    convert_element_type x15 -> x3, local copies, waits for them, and re-layouts: 39.9 us -> 0.19 us  [body(): vectors.transpose(1, 0, 2).reshape(vector_count, width).astype(jnp.float32)]
    unnamed x150 -> x13, local copies, waits for them, and re-layouts: 28.8 us -> 1.66 us
  transfers between devices with their start and end apart: 13 -> 4, of which waited for: 10 -> 1; matrix products, arithmetic and copies ran while one was open for 16% -> 4% of each run, Pallas kernels for 0% -> 46%
where the time goes in v2:
time: 498 us; the launch traced here: 493 us
  Pallas kernels  393 us (79%)
  waiting for transfers between devices  50.3 us (10%)
  other arithmetic  21.2 us (4%)
  between operations  14.3 us (3%)
  local copies, waits for them, and re-layouts  13.9 us (3%)
    pallas_call x1, Pallas kernels, reduce_grads(): pl.pallas_call(functools.partial(reduce_kernel, parts, bits), out_shape=[...  123 us
    pallas_call x1, Pallas kernels, gather_weights(): pl.pallas_call(functools.partial(gather_kernel, parts, bits), out_shape=[...  99.1 us
    pallas_call x2, Pallas kernels, attend_back(): pl.pallas_call(functools.partial(attend_back_kernel, micro), grid_spec=pl...  54 us
    all_gather x2, waiting for transfers between devices, body(): lax.all_gather(jnp.concatenate(outs[m * per_micro:(m + 1) * per_micro], a...  49.1 us
    pallas_call x2, Pallas kernels, attend(): pl.pallas_call(functools.partial(attend_kernel, micro), grid_spec=pltpu.P...  32.3 us
    pallas_call x2, Pallas kernels, ffn(): pl.pallas_call(functools.partial(ffn_kernel, micro), grid_spec=pltpu.Pref...  31.2 us
    pallas_call x2, Pallas kernels, ffn_back(): pl.pallas_call(ffn_back_kernel, grid=(parts,), in_specs=[whole(slot_count...  26.9 us
    pallas_call x1, Pallas kernels, weight_grads(): pl.pallas_call(functools.partial(weight_grads_kernel, blocks), grid_spec=...  26.5 us
  transfers between devices with their start and end apart: 4, of which 1 were waited for; matrix products, arithmetic and copies ran while one was open for 4% of the time, Pallas kernels for 46%

profile of v2, /device:TPU:0, one launch (start us, length us, event | category | flops | bytes accessed | tf_op | source)
XLA Modules:
  0.0 493.1 jit_solution(3208155117078419800)
XLA Ops:
  7.2 0.0 all-gather.9.cloned.1.call-start
  7.2 0.9 slice_bitcast_fusion.3
  8.1 0.9 copy.37
  9.0 0.8 fusion.10
  9.8 0.7 slice.186
  10.5 0.7 pad_maximum_fusion.5
  11.2 0.1 reshape.37
  11.3 0.7 broadcast_in_dim.7
  12.0 0.1 fusion.6
  12.1 0.1 concatenate.47
  12.2 0.6 pad_maximum_fusion.4.small
  12.8 0.1 concatenate.44
  13.0 1.8 pad_maximum_fusion.2.own
  14.8 99.1 %gather_weights.1 = (bf16[3,4,2,2,2,96,768]{6,5,4,3,2,1,0:T(8,128)(2,1)}, bf16[2,2,2,16,768]{4,3,2,1,0:T(8,128)(2,1)}, bf16[4,16,768]{2,1,0:T(8,128)(2,1)}) custom-call(bf16[3,96,768]{2,1,0:T(8,128)(2,1)} %pad_maximum_fusion.2.own, bf16[2,16,768]{2,1,0:T(8,128)(2,1)} %pad_maximum_fusion.4.small), custom_call_target="tpu_custom_call" | custom-call | tf_op jit(solution)/shard_map/gather_weights/pallas_call | solution.py:582
  113.8 0.9 slice.230
  114.8 0.1 convert_element_type.25
  114.9 0.1 convert_element_type.27
  115.0 0.6 pad_convert_fusion.vec_ref.refs_14_
  115.6 1.5 slice_convert_fusion
  117.1 16.1 %attend.2 = (f32[512,768]{1,0:T(8,128)}, f32[512,128]{1,0:T(8,128)}, bf16[4,512,768]{2,1,0:T(8,128)(2,1)}, bf16[12,512,512]{2,1,0:T(8,128)(2,1)}, bf16[4,512,256]{2,1,0:T(8,128)(2,1)}) custom-call(s32[1]{0:T(128)} %bitcast.place, s32[2,4]{1,0:T(2,128)} %bucket.11, s32[2,4,4]{2,1,0:T(4,128)} %lengths.11, s32[2,4]{1,0:T(2,128)} %counts.11, ...), custom_call_target="tpu_custom_call" | custom-call | tf_op jit(solution)/shard_map/attend/pallas_call | solution.py:246
  133.2 15.6 %ffn.2 = (bf16[4,512,768]{2,1,0:T(8,128)(2,1)}, bf16[4,512,768]{2,1,0:T(8,128)(2,1)}, bf16[512,768]{1,0:T(8,128)(2,1)}, f32[512,768]{1,0:T(8,128)}, bf16[512,768]{1,0:T(8,128)(2,1)}, /*index=5*/f32[8,768]{1,0:T(8,128)}) custom-call(s32[1]{0:T(128)} %bitcast.place, s32[2,4]{1,0:T(2,128)} %bucket.11, s32[2,4,4]{2,1,0:T(4,128)} %lengths.11, s32[2,4]{1,0:T(2,128)} %counts.11, ...), custom_call_target="tpu_custom_call" | custom-call | tf_op jit(solution)/shard_map/ffn/pallas_call | solution.py:283
  148.7 13.4 %ffn_back.2 = (bf16[4,512,768]{2,1,0:T(8,128)(2,1)}, f32[512,768]{1,0:T(8,128)}, bf16[512,768]{1,0:T(8,128)(2,1)}, f32[4,8,768]{2,1,0:T(8,128)}, f32[8,768]{1,0:T(8,128)}) custom-call(f32[512,768]{1,0:T(8,128)} %get-tuple-element.60.second_ref, bf16[512,768]{1,0:T(8,128)(2,1)} %get-tuple-element.61.second_low_ref.refs_2_, ...), custom_call_target="tpu_custom_call" | custom-call | tf_op jit(solution)/shard_map/ffn_back/pallas_call | solution.py:317
  162.2 22.3 %attend_back.2 = (bf16[4,512,768]{2,1,0:T(8,128)(2,1)}, bf16[512,768]{1,0:T(8,128)(2,1)}, f32[4,8,768]{2,1,0:T(8,128)}) custom-call(s32[1]{0:T(128)} %bitcast.place, s32[2,4]{1,0:T(2,128)} %bucket.11, s32[2,4,4]{2,1,0:T(4,128)} %lengths.11, s32[2,4]{1,0:T(2,128)} %counts.11, f32[512,768]{1,0:T(8,128)} %get-tuple-element.64.hidden_ref, ...), custom_call_target="tpu_custom_call" | custom-call | tf_op jit(solution)/shard_map/attend_back/pallas_call | solution.py:351
  184.5 0.0 all-gather.9.cloned.1.call-update
  184.6 0.0 all-gather.11.cloned.1.call-start
  184.6 16.1 %attend.3 = (f32[512,768]{1,0:T(8,128)}, f32[512,128]{1,0:T(8,128)}, bf16[4,512,768]{2,1,0:T(8,128)(2,1)}, bf16[12,512,512]{2,1,0:T(8,128)(2,1)}, bf16[4,512,256]{2,1,0:T(8,128)(2,1)}) custom-call(s32[1]{0:T(128)} %bitcast.place, s32[2,4]{1,0:T(2,128)} %bucket.11, s32[2,4,4]{2,1,0:T(4,128)} %lengths.11, s32[2,4]{1,0:T(2,128)} %counts.11, ...), custom_call_target="tpu_custom_call" | custom-call | tf_op jit(solution)/shard_map/attend/pallas_call | solution.py:246
  200.7 15.6 %ffn.3 = (bf16[4,512,768]{2,1,0:T(8,128)(2,1)}, bf16[4,512,768]{2,1,0:T(8,128)(2,1)}, bf16[512,768]{1,0:T(8,128)(2,1)}, f32[512,768]{1,0:T(8,128)}, bf16[512,768]{1,0:T(8,128)(2,1)}, /*index=5*/f32[8,768]{1,0:T(8,128)}) custom-call(s32[1]{0:T(128)} %bitcast.place, s32[2,4]{1,0:T(2,128)} %bucket.11, s32[2,4,4]{2,1,0:T(4,128)} %lengths.11, s32[2,4]{1,0:T(2,128)} %counts.11, ...), custom_call_target="tpu_custom_call" | custom-call | tf_op jit(solution)/shard_map/ffn/pallas_call | solution.py:283
  216.4 13.5 %ffn_back.3 = (bf16[4,512,768]{2,1,0:T(8,128)(2,1)}, f32[512,768]{1,0:T(8,128)}, bf16[512,768]{1,0:T(8,128)(2,1)}, f32[4,8,768]{2,1,0:T(8,128)}, f32[8,768]{1,0:T(8,128)}) custom-call(f32[512,768]{1,0:T(8,128)} %get-tuple-element.70.second_ref, bf16[512,768]{1,0:T(8,128)(2,1)} %get-tuple-element.71.second_low_ref.refs_3_, ...), custom_call_target="tpu_custom_call" | custom-call | tf_op jit(solution)/shard_map/ffn_back/pallas_call | solution.py:317
  229.9 0.0 copy-start.1
  229.9 0.0 copy-start.3
  229.9 0.0 copy-start
  229.9 0.0 copy-start.2
  229.9 31.7 %attend_back.3 = (bf16[4,512,768]{2,1,0:T(8,128)(2,1)}, bf16[512,768]{1,0:T(8,128)(2,1)}, f32[4,8,768]{2,1,0:T(8,128)}) custom-call(s32[1]{0:T(128)} %bitcast.place, s32[2,4]{1,0:T(2,128)} %bucket.11, s32[2,4,4]{2,1,0:T(4,128)} %lengths.11, s32[2,4]{1,0:T(2,128)} %counts.11, f32[512,768]{1,0:T(8,128)} %get-tuple-element.74.hidden_ref, ...), custom_call_target="tpu_custom_call" | custom-call | tf_op jit(solution)/shard_map/attend_back/pallas_call | solution.py:351
  261.6 0.0 all-gather.11.cloned.1.call-update
  261.6 0.0 all-gather.5.cloned.1.call-start
  261.7 0.7 all-gather.5.cloned.1.call-update
  262.4 0.0 all-gather.7.cloned.1.call-start
  262.4 0.5 all-gather.7.cloned.1.call-update
  262.9 1.0 slice_add_fusion
  263.9 1.0 slice_add_fusion.1
  264.9 0.0 copy-done.1
  264.9 0.0 copy-done.3
  264.9 0.0 copy-done
  265.0 0.2 concatenate.49
  265.1 0.6 pad.22.small
  265.8 26.5 %weight_grads.1 = bf16[3,4,768,768]{3,2,1,0:T(8,128)(2,1)} custom-call(s32[1]{0:T(128)} %bitcast.place, f32[512,768]{1,0:T(8,128)} %get-tuple-element.56.normed_ref.refs_0_, f32[512,768]{1,0:T(8,128)} %get-tuple-element.58.normed_ref.refs_1_, bf16[512,768]{1,0:T(8,128)(2,1)} %get-tuple-element.61.second_low_ref.refs_2_, ...), custom_call_target="tpu_custom_call" | custom-call | tf_op jit(solution)/shard_map/weight_grads/pallas_call | solution.py:417
  292.3 123.2 %reduce_grads.1 = (f32[3,96,768]{2,1,0:T(8,128)}, f32[16,768]{1,0:T(8,128)}) custom-call(bf16[3,4,2,2,2,96,768]{6,5,4,3,2,1,0:T(8,128)(2,1)} %bitcast.61, f32[16,768]{1,0:T(8,128)} %pad.22.small), custom_call_target="tpu_custom_call" | custom-call | tf_op jit(solution)/shard_map/reduce_grads/pallas_call | solution.py:768
  415.5 0.7 slice.217
  416.2 0.1 constant_dynamic-slice_fusion.1
  416.3 0.6 slice.219
  416.9 0.6 slice.218
  417.5 2.0 slice_bitcast_fusion
  419.5 0.1 fusion.5
  419.6 0.7 copy.42
  420.4 0.7 dynamic-slice.3
  421.1 1.3 dynamic-slice_reduce_fusion
  422.5 0.8 constant_dynamic-slice_fusion
  423.2 0.7 maximum_maximum_fusion
  423.9 0.1 maximum_bitcast_fusion
  424.0 0.1 maximum_bitcast_fusion.1
  424.1 0.7 pad_maximum_fusion.3
  424.8 6.4 %pad_maximum_fusion.1 = bf16[2,2048,768]{2,1,0:T(8,128)(2,1)} fusion(bf16[1,2048,768]{2,1,0:T(8,128)(2,1)} %bitcast.63, bf16[1,2048,768]{2,1,0:T(8,128)(2,1)} %bitcast.62), kind=kLoop, calls=%fused_computation.1 | loop fusion | flops 3145728 | bytes 12582912 | tf_op jit(solution)/shard_map/stack | solution.py:892
  431.2 49.1 %all-gather.7.cloned.1.call-done = bf16[2048,768]{1,0:T(8,128)(2,1)} async-done(((bf16[512,768]{1,0:T(8,128)(2,1)}), bf16[2048,768]{1,0:T(8,128)(2,1)}) %all-gather.7.cloned.1.call-update) | async-done | bytes 3145744 | tf_op jit(solution)/shard_map/all_gather | solution.py:858
  480.3 6.1 %pad_maximum_fusion = bf16[2,2048,768]{2,1,0:T(8,128)(2,1)} fusion(bf16[1,2048,768]{2,1,0:T(8,128)(2,1)} %bitcast.65, bf16[1,2048,768]{2,1,0:T(8,128)(2,1)} %bitcast.64), kind=kLoop, calls=%fused_computation | loop fusion | flops 3145728 | bytes 12582912 | tf_op jit(solution)/shard_map/stack | solution.py:891
  (22 shorter events, 0.1 us)
Async XLA Ops:
  7.2 417.6 %all-gather.9.cloned.1.call-start = ((), (), s32[]{:S(2)}) async-start(), calls=%async_computation.2 | async-start | bytes 3932160 | tf_op jit(solution)/shard_map/all_gather | solution.py:870
  184.6 240.3 %all-gather.11.cloned.1.call-start = ((), (), s32[]{:S(2)}) async-start(), calls=%async_computation.3 | async-start | bytes 3932160 | tf_op jit(solution)/shard_map/all_gather | solution.py:870
  229.9 35.0 %copy-start.1 = (f32[8,768]{1,0:T(8,128)S(1)}, f32[8,768]{1,0:T(8,128)}, u32[]{:S(2)}) copy-start(f32[8,768]{1,0:T(8,128)} %get-tuple-element.86) | copy-start | bytes 73732
  229.9 35.0 %copy-start.3 = (f32[8,768]{1,0:T(8,128)S(1)}, f32[8,768]{1,0:T(8,128)}, u32[]{:S(2)}) copy-start(f32[8,768]{1,0:T(8,128)} %get-tuple-element.87) | copy-start | bytes 73732
  229.9 35.0 %copy-start = (f32[8,768]{1,0:T(8,128)S(1)}, f32[8,768]{1,0:T(8,128)}, u32[]{:S(2)}) copy-start(f32[8,768]{1,0:T(8,128)} %get-tuple-element.88) | copy-start | bytes 73732
  229.9 35.0 %copy-start.2 = (f32[8,768]{1,0:T(8,128)S(1)}, f32[8,768]{1,0:T(8,128)}, u32[]{:S(2)}) copy-start(f32[8,768]{1,0:T(8,128)} %get-tuple-element.89) | copy-start | bytes 73732
  261.6 169.6 %all-gather.5.cloned.1.call-start = ((), (), s32[]{:S(2)}) async-start(), calls=%async_computation | async-start | bytes 3932160 | tf_op jit(solution)/shard_map/all_gather | solution.py:858
  262.4 217.9 %all-gather.7.cloned.1.call-start = ((), (), s32[]{:S(2)}) async-start(), calls=%async_computation.1 | async-start | bytes 3932160 | tf_op jit(solution)/shard_map/all_gather | solution.py:858
Sparse Core Ops, SparseCore 0:
  184.7 61.2 all-gather.8
  261.7 61.2 all-gather.10
  324.6 88.1 all-gather.4
  414.3 65.9 all-gather.6
